TPU v7x, 32 devices: a whole 2x2x4 slice. The times are simulated.
32 devices in a mesh: kv: 2 (over y), ex: 16 (over z, x, core).
Axes of the slice: x: 2, y: 2, z: 4, core: 2. Of those that a mesh axis runs over, the one named last changes fastest.
Arguments:
- x_tokens: bfloat16 [16, 576, 2048], P('ex'), may hold values from -6 to 6
- attn_gain: float32 [2048], replicated, may hold values from 0.1 to 1.9
- w_qkv: bfloat16 [2048, 3, 2048], P(None, None, 'kv'), may hold values from -1 to 1
- w_out: bfloat16 [2048, 2048], P('kv'), may hold values from -0.125 to 0.125
- cache: bfloat16 [32, 2, 512, 2048], P('ex', None, None, 'kv'), may hold values from -6 to 6
- cache_len: int32 [32], P('ex'), may hold values from 1 to 512, 8192 in all
- moe_gain: float32 [2048], replicated, may hold values from 0.1 to 1.9
- w_trainer: float32 [16, 3, 2048, 1024], P(None, None, 'ex', 'kv'), may hold values from -0.125 to 0.125
- expert_ids: int32 [16, 576, 8], P('ex', 'kv'), may hold values from 0 to 15, all different within a row; in each aligned block of 288 rows (0 to 287, 288 to 575, ..., all dimensions but the last counted through in order) at most 230 rows name the same one
- route_probs: float32 [16, 576, 8], P('ex', 'kv'), may hold values from 0.05 to 1
Outputs:
- layer_out: bfloat16 [16, 576, 2048], P('ex', 'kv')
Inputs may be any that keep to these rules, and one draw needn't show every extreme that they name: `expert_ids`: in each aligned block of 288 tokens, no expert is named by more than 230 of them; each token names 8 different experts.
All inputs are finite; a program needn't handle non-finite values. No bound on the sum of `cache_len` on one device may be relied on, other than what follows from the above.
Results may differ from a plain program's by a relative error of at most 0.0055.
Values may be sent and summed in bfloat16 or wider, within the bound.
No kernel may reach another device: no remote copies, remote signals or barrier semaphores. Data moves between devices by JAX's collectives and lax.ppermute only.
A program may use at most 192 MiB of HBM per device.

v0:
```python
import functools
import math

import jax
import jax.numpy as jnp
from jax import lax
from jax.experimental import pallas as pl
from jax.experimental.pallas import tpu as pltpu
from jax.sharding import PartitionSpec as P

HD = 128
TOPK = 8
PLEN = 512
REQ_DEV = 2
QB = 32
CMAX = 512


def rms_scale(rows, gain):
    values = rows.astype(jnp.float32)
    scale = lax.rsqrt(jnp.mean(values * values, axis=-1, keepdims=True) + 1e-06)
    return values * scale * gain


def attention_kernel(scale, len_ref, x_ref, gain_ref, w_ref, cache_ref, w_out_ref, out_ref, normed):
    @pl.when(pl.program_id(0) == 0)
    def _():
        normed[...] = rms_scale(x_ref[...], gain_ref[...]).astype(jnp.bfloat16)
        out_ref[...] = jnp.zeros_like(out_ref)

    rows = normed[...]
    query, keys, values = (
        jnp.dot(rows, w_ref[j], preferred_element_type=jnp.float32).astype(jnp.bfloat16)
        for j in range(3)
    )

    def scores_of(q, k):
        return scale * lax.dot_general(
            q, k, (((1,), (1,)), ((), ())), preferred_element_type=jnp.float32
        )

    def mix(weights, v):
        return jnp.dot(weights.astype(jnp.bfloat16), v, preferred_element_type=jnp.float32)

    heads = []
    for head in range(query.shape[1] // HD):
        cut = slice(head * HD, (head + 1) * HD)
        q, k, v = query[:, cut], keys[:, cut], values[:, cut]
        scores = scores_of(q[:PLEN], k[:PLEN])
        weights = jnp.exp(scores - jnp.max(scores, axis=-1, keepdims=True))
        total = jnp.sum(weights, axis=-1, keepdims=True)
        outs = [(mix(weights, v[:PLEN]) / total).astype(jnp.bfloat16)]
        for request in range(REQ_DEV):
            own = slice(PLEN + request * QB, PLEN + (request + 1) * QB)
            fresh = scores_of(q[own], k[own])
            stored = scores_of(q[own], cache_ref[request, 0, :, cut])
            slots = lax.broadcasted_iota(jnp.int32, stored.shape, 1)
            stored = jnp.where(slots < len_ref[request], stored, -1e30)
            top = jnp.maximum(
                jnp.max(fresh, axis=-1, keepdims=True), jnp.max(stored, axis=-1, keepdims=True)
            )
            fresh, stored = jnp.exp(fresh - top), jnp.exp(stored - top)
            total = jnp.sum(fresh, axis=-1, keepdims=True) + jnp.sum(stored, axis=-1, keepdims=True)
            mixed = mix(fresh, v[own]) + mix(stored, cache_ref[request, 1, :, cut])
            outs.append((mixed / total).astype(jnp.bfloat16))
        heads.append(jnp.concatenate(outs, axis=0))
    out_ref[...] += jnp.dot(
        jnp.concatenate(heads, axis=1), w_out_ref[...], preferred_element_type=jnp.float32
    )


def attention(rows, gain, w_qkv, cache, cache_len, w_out):
    count, width = rows.shape
    units = w_qkv.shape[2]
    block = min(2 * HD, units)
    return pl.pallas_call(
        functools.partial(attention_kernel, 1.0 / math.sqrt(HD)),
        grid=(units // block,),
        in_specs=[
            pl.BlockSpec(memory_space=pltpu.SMEM),
            pl.BlockSpec((count, width), lambda i: (0, 0)),
            pl.BlockSpec((1, width), lambda i: (0, 0)),
            pl.BlockSpec((3, width, block), lambda i: (0, 0, i)),
            pl.BlockSpec((REQ_DEV, 2, CMAX, block), lambda i: (0, 0, 0, i)),
            pl.BlockSpec((block, width), lambda i: (i, 0)),
        ],
        out_specs=pl.BlockSpec((count, width), lambda i: (0, 0)),
        out_shape=jax.ShapeDtypeStruct((count, width), jnp.float32),
        scratch_shapes=[pltpu.VMEM((count, width), jnp.bfloat16)],
        compiler_params=pltpu.CompilerParams(vmem_limit_bytes=38 * 1024 * 1024),
        cost_estimate=pl.CostEstimate(
            flops=8 * count * width * units + 4 * PLEN * PLEN * units,
            bytes_accessed=8 * width * units + 6 * count * width,
            transcendentals=PLEN * PLEN * units // HD,
        ),
        name="attention",
    )(cache_len, rows, gain[None], jnp.transpose(w_qkv, (1, 0, 2)), cache, w_out)


def share_columns(share):
    high = share.astype(jnp.bfloat16)
    low = (share - high.astype(jnp.float32)).astype(jnp.bfloat16)
    spare = -2 * share.shape[1] % 128
    return jnp.concatenate([high, low, jnp.zeros((share.shape[0], spare), jnp.bfloat16)], axis=1)


def hidden_kernel(experts, width, me_ref, *refs):
    x_refs, weight_refs, out_refs = refs[:2], refs[2:-2], refs[-2:]
    units = weight_refs[0].shape[2]
    me = me_ref[0]
    for x_ref, out_ref in zip(x_refs, out_refs):
        extra = x_ref[:, width:].astype(jnp.float32)
        lanes = lax.broadcasted_iota(jnp.int32, extra.shape, 1)
        mine = (lanes == me) | (lanes == me + experts)
        share = jnp.sum(jnp.where(mine, extra, 0.0), axis=-1, keepdims=True)
        for part in range(len(weight_refs) // 2):
            gate_w, up_w = (r[...].reshape(width, units) for r in weight_refs[2 * part : 2 * part + 2])
            x = x_ref[:, :width]
            gate = jnp.dot(x, gate_w, preferred_element_type=jnp.float32)
            up = jnp.dot(x, up_w, preferred_element_type=jnp.float32)
            gate = 0.5 * gate
            out_ref[:, part * units : (part + 1) * units] = (
                (gate + gate * jnp.tanh(gate)) * (up * share)
            ).astype(jnp.bfloat16)


def expert_hidden(experts, me, blocks, weights):
    count = blocks[0].shape[0]
    sources, slice_width, units = weights[0].shape
    width, hidden = sources * slice_width, units * len(weights) // 2
    vmem = pl.BlockSpec(memory_space=pltpu.VMEM)
    out = jax.ShapeDtypeStruct((count, hidden), jnp.bfloat16)
    return pl.pallas_call(
        functools.partial(hidden_kernel, experts, width),
        in_specs=[pl.BlockSpec(memory_space=pltpu.SMEM)] + [vmem] * (2 + len(weights)),
        out_specs=[vmem] * 2,
        out_shape=[out, out],
        compiler_params=pltpu.CompilerParams(vmem_limit_bytes=8 * 1024 * 1024),
        cost_estimate=pl.CostEstimate(
            flops=8 * count * width * hidden,
            bytes_accessed=4 * count * (width + hidden) + 4 * width * hidden,
            transcendentals=2 * count * hidden,
        ),
        name="expert_hidden",
    )(me, *blocks, *weights)


def down_kernel(*refs):
    hidden_refs, weight_refs, out_refs = refs[:2], refs[2:-2], refs[-2:]
    sources, slice_width, units = weight_refs[0].shape
    group = max(1, min(sources, 1024 // slice_width))
    for hidden_ref, out_ref in zip(hidden_refs, out_refs):
        for first in range(0, sources, group):
            total = None
            for part, weight_ref in enumerate(weight_refs):
                term = lax.dot_general(
                    hidden_ref[:, part * units : (part + 1) * units],
                    weight_ref[first : first + group].reshape(group * slice_width, units),
                    (((1,), (1,)), ((), ())),
                    preferred_element_type=jnp.float32,
                )
                total = term if total is None else total + term
            cut = slice(first * slice_width, (first + group) * slice_width)
            out_ref[:, cut] = total.astype(jnp.bfloat16)


def expert_down(hiddens, weights):
    count, hidden = hiddens[0].shape
    width = weights[0].shape[0] * weights[0].shape[1]
    vmem = pl.BlockSpec(memory_space=pltpu.VMEM)
    out = jax.ShapeDtypeStruct((count, width), jnp.bfloat16)
    return pl.pallas_call(
        down_kernel,
        in_specs=[vmem] * (2 + len(weights)),
        out_specs=[vmem] * 2,
        out_shape=[out, out],
        compiler_params=pltpu.CompilerParams(vmem_limit_bytes=8 * 1024 * 1024),
        cost_estimate=pl.CostEstimate(
            flops=4 * count * width * hidden,
            bytes_accessed=4 * count * (width + hidden) + 2 * width * hidden,
            transcendentals=0,
        ),
        name="expert_down",
    )(*hiddens, *weights)


def sum_kernel(cut, refs):
    total = refs[0][:, cut].astype(jnp.float32) + refs[1][:, cut].astype(jnp.float32)
    for ref in refs[2:-1]:
        total = total + ref[...].astype(jnp.float32)
    refs[-1][...] = total.astype(jnp.bfloat16)


def add_terms(cut, keep, got, running):
    terms = [keep, got] + ([] if running is None else [running])
    columns = cut.stop - cut.start
    vmem = pl.BlockSpec(memory_space=pltpu.VMEM)
    return pl.pallas_call(
        lambda *refs: sum_kernel(cut, refs),
        in_specs=[vmem] * len(terms),
        out_specs=vmem,
        out_shape=jax.ShapeDtypeStruct((keep.shape[0], columns), jnp.bfloat16),
        compiler_params=pltpu.CompilerParams(vmem_limit_bytes=8 * 1024 * 1024),
        cost_estimate=pl.CostEstimate(
            flops=2 * keep.shape[0] * columns,
            bytes_accessed=8 * keep.shape[0] * columns,
            transcendentals=0,
        ),
        name="add_terms",
    )(*terms)


def chip_ring(chips):
    rows = 4
    columns = chips // rows
    if chips % rows or columns < 2:
        return list(range(chips))
    order = [z * columns for z in range(rows)]
    for turn, z in enumerate(reversed(range(rows))):
        line = [z * columns + x for x in range(1, columns)]
        order += line if turn % 2 == 0 else line[::-1]
    return order


def on_device(
    x_tokens,
    attn_gain,
    w_qkv,
    w_out,
    cache,
    cache_len,
    moe_gain,
    w_trainer,
    expert_ids,
    route_probs,
):
    kv, ex = lax.axis_size("kv"), lax.axis_size("ex")
    me, me_kv = lax.axis_index("ex"), lax.axis_index("kv")
    experts = w_trainer.shape[0]

    def over_experts(part):
        return lax.all_to_all(part, "ex", split_axis=0, concat_axis=0, tiled=True)

    def over_kv(part):
        return [
            lax.ppermute(part, "kv", [(i, (i + turn) % kv) for i in range(kv)])
            for turn in range(1, kv)
        ]

    probs = route_probs[0]
    share = probs / jnp.sum(probs, axis=-1, keepdims=True)
    named = expert_ids[0][:, :, None] == jnp.arange(experts, dtype=jnp.int32)[None, None, :]
    factor = jnp.sum(jnp.where(named, share[:, :, None], 0.0), axis=1)
    factor = share_columns(factor)

    rows = x_tokens[0]
    row_count = rows.shape[0]
    rows_dev = row_count // kv
    gate = w_trainer[:, 0].astype(jnp.bfloat16)
    gate, rest = lax.optimization_barrier((gate, w_trainer))
    up, down = (rest[:, kind].astype(jnp.bfloat16) for kind in (1, 2))
    gate = over_experts(gate)
    mixed = attention(rows, attn_gain, w_qkv, cache, cache_len, w_out)
    mixed, gate, up, down = lax.optimization_barrier((mixed, gate, up, down))
    gates = over_kv(gate)
    up = over_experts(up)
    mixed = mixed.reshape(kv, rows_dev, mixed.shape[1])

    def rows_of(part):
        return lax.dynamic_index_in_dim(mixed, part, 0, keepdims=False)

    own_rows = lax.dynamic_slice_in_dim(rows, me_kv * rows_dev, rows_dev, 0)
    resid = own_rows.astype(jnp.float32) + rows_of(me_kv)
    for turn in range(1, kv):
        sent = rows_of(lax.rem(me_kv + turn, kv)).astype(jnp.bfloat16)
        sent = lax.ppermute(sent, "kv", [(i, (i + turn) % kv) for i in range(kv)])
        resid = resid + sent.astype(jnp.float32)
    resid, up, down = lax.optimization_barrier((resid, up, down))
    ups = over_kv(up)
    down = over_experts(down)
    moe_in = rms_scale(resid, moe_gain).astype(jnp.bfloat16)
    moe_in = jnp.concatenate([moe_in, factor], axis=1)
    moe_in, gates = lax.optimization_barrier((moe_in, gates))

    cores = 2
    order = chip_ring(ex // cores)
    chips = len(order)
    half = rows_dev // 2
    core = lax.rem(me, cores)
    ring, swap = [], [(i, i ^ 1) for i in range(ex)]
    for spot, chip in enumerate(order):
        for c in range(cores):
            here = chip * cores + c
            ring.append((here, order[(spot + 1 - 2 * c) % chips] * cores + c))

    def half_of(array, which):
        return lax.dynamic_slice_in_dim(array, which * half, half, 0)

    got = lax.ppermute(half_of(moe_in, 1 - core), "ex", swap)
    held = jnp.concatenate([half_of(moe_in, core), got], axis=0)
    first_weights = [gate, up]
    due = {3: [0, 1], 4: [2, 3], 5: [4], 6: [5], 7: [6]}
    blocks, hiddens = [held], {}

    def hidden_of(step):
        other = lax.ppermute(blocks[step], "ex", swap)
        return expert_hidden(experts, me[None], [blocks[step], other], first_weights)

    for step in range(1, chips):
        held = lax.ppermute(held, "ex", ring)
        if step == 1:
            held, down = lax.optimization_barrier((held, down))
            downs = over_kv(down)
        if step == 2:
            held, ups = lax.optimization_barrier((held, ups))
            for pair in zip(gates, ups):
                first_weights += pair
        blocks.append(held)
        for early in due.get(step, []):
            hiddens[early] = hidden_of(early)
            held, hiddens[early] = lax.optimization_barrier((held, hiddens[early]))
        if step == min(3, chips - 1):
            held, downs = lax.optimization_barrier((held, downs))
        blocks[step] = held
    for step in range(chips):
        if step not in hiddens:
            hiddens[step] = hidden_of(step)
    hiddens = [hiddens[step] for step in range(chips)]
    keeps, gots = [], []
    for pair in hiddens:
        keep, give = expert_down(pair, [down] + downs)
        keeps.append(keep)
        gots.append(lax.ppermute(give, "ex", swap))

    width = w_out.shape[1]
    sums = []
    for cut in (slice(0, width // 2), slice(width // 2, width)):
        running = None
        for step in list(range(1, chips)) + [0]:
            running = add_terms(cut, keeps[step], gots[step], running)
            if step:
                running = lax.ppermute(running, "ex", ring)
        sums.append(running)
    running = jnp.concatenate(sums, axis=1)
    got = lax.ppermute(running[half:], "ex", swap)
    moe_out = jnp.where(
        core == 0,
        jnp.concatenate([running[:half], got], axis=0),
        jnp.concatenate([got, running[:half]], axis=0),
    )
    return (resid + moe_out.astype(jnp.float32)).astype(jnp.bfloat16)[None]


def solution(mesh):
    return jax.shard_map(
        on_device,
        mesh=mesh,
        in_specs=(
            P("ex", None, None),
            P(),
            P(None, None, "kv"),
            P("kv", None),
            P("ex", None, None, "kv"),
            P("ex"),
            P(),
            P(None, None, "ex", "kv"),
            P("ex", "kv", None),
            P("ex", "kv", None),
        ),
        out_specs=P("ex", "kv", None),
        check_vma=False,
    )
```

profile of v0, /device:TPU:0, one launch (start us, length us, event | category | flops | bytes accessed | tf_op | source)
XLA Modules:
  0.0 413.6 jit_solution(15634729327423846598)
XLA Ops:
  0.0 3.8 fusion
  3.8 7.4 %all-to-all-start = ((bf16[16,128,512]{2,1,0:T(8,128)(2,1)}), bf16[16,128,512]{2,1,0:T(8,128)(2,1)S(1)}, u32[]{:S(2)}, u32[]{:S(2)}) async-start(bf16[16,128,512]{2,1,0:T(8,128)(2,1)} %fusion), calls=%async_computation | async-start | bytes 4194304 | tf_op jit(solution)/shard_map/all_to_all | solution.py:242
  11.2 6.3 %slice_bitcast_fusion = (bf16[16,128,512]{2,1,0:T(8,128)(2,1)}, bf16[16,128,512]{2,1,0:T(8,128)(2,1)}) fusion(f32[16,3,128,512]{3,2,1,0:T(8,128)} %param.17), kind=kLoop, calls=%fused_computation.8 | loop fusion | bytes 8388608 | tf_op jit(solution)/shard_map/convert_element_type | solution.py:261
  17.6 2.2 copy-done.3
  19.7 23.9 %attention.1 = f32[576,2048]{1,0:T(8,128)S(1)} custom-call(s32[2]{0:T(128)S(1)} %copy-done.5, bf16[576,2048]{1,0:T(8,128)(2,1)S(1)} %bitcast.22, f32[1,2048]{1,0:T(1,128)S(1)} %bitcast.23, bf16[3,2048,1024]{2,1,0:T(8,128)(2,1)} %bitcast.25, bf16[2,2,512,1024]{3,2,1,0:T(8,128)(2,1)S(1)} %copy-done.2, bf16[1024,2048]{1,0:T(8,128)(2,1)S(1)} %copy-done.3), custom_call_target="tpu_custom_call" | custom-call | flops 10737418240 | bytes 23855104 | tf_op jit(solution)/shard_map/attention/pallas_call | solution.py:76
  43.6 2.2 copy-done
  45.8 6.5 %all-to-all-done.refs_2_ = bf16[16,128,512]{2,1,0:T(8,128)(2,1)S(1)} async-done(((bf16[16,128,512]{2,1,0:T(8,128)(2,1)}), bf16[16,128,512]{2,1,0:T(8,128)(2,1)S(1)}, u32[]{:S(2)}, u32[]{:S(2)}) %all-to-all-start) | async-done | bytes 2097184 | tf_op jit(solution)/shard_map/all_to_all | solution.py:242
  52.3 11.3 %all-to-all-start.1 = ((bf16[16,128,512]{2,1,0:T(8,128)(2,1)}), bf16[16,128,512]{2,1,0:T(8,128)(2,1)}, u32[]{:S(2)}, u32[]{:S(2)}) async-start(bf16[16,128,512]{2,1,0:T(8,128)(2,1)} %get-tuple-element.78), calls=%async_computation.1 | async-start | bytes 4194304 | tf_op jit(solution)/shard_map/all_to_all | solution.py:242
  67.5 26.8 %collective-permute-done = bf16[288,2048]{1,0:T(8,128)(2,1)} collective-permute-done((bf16[288,2048]{1,0:T(8,128)(2,1)S(1)}, bf16[288,2048]{1,0:T(8,128)(2,1)}, u32[]{:S(2)}, u32[]{:S(2)}) %collective-permute-start) | collective-permute-done | bytes 1179680 | tf_op jit(solution)/shard_map/ppermute | solution.py:276
  94.4 4.3 %bitcast_add_fusion = f32[288,2048]{1,0:T(8,128)} fusion(bf16[288,2048]{1,0:T(8,128)(2,1)} %collective-permute-done, f32[2,288,2048]{2,1,0:T(8,128)} %bitcast.21, s32[]{:T(128)S(6)} %select_n.29, bf16[1,576,2048]{2,1,0:T(8,128)(2,1)} %param.10, s32[]{:T(128)S(6)} %select_n.28), kind=kLoop, calls=%fused_computation.2 | loop fusion | flops 2359296 | bytes 7077896 | tf_op jit(solution)/shard_map/add | solution.py:277
  98.7 6.0 %all-to-all-done.1.refs_3_ = bf16[16,128,512]{2,1,0:T(8,128)(2,1)} async-done(((bf16[16,128,512]{2,1,0:T(8,128)(2,1)}), bf16[16,128,512]{2,1,0:T(8,128)(2,1)}, u32[]{:S(2)}, u32[]{:S(2)}) %all-to-all-start.1) | async-done | bytes 2097184 | tf_op jit(solution)/shard_map/all_to_all | solution.py:242
  104.7 11.3 %all-to-all-start.2 = ((bf16[16,128,512]{2,1,0:T(8,128)(2,1)}), bf16[16,128,512]{2,1,0:T(8,128)(2,1)}, u32[]{:S(2)}, u32[]{:S(2)}) async-start(bf16[16,128,512]{2,1,0:T(8,128)(2,1)} %get-tuple-element.83), calls=%async_computation.2 | async-start | bytes 4194304 | tf_op jit(solution)/shard_map/all_to_all | solution.py:242
  120.7 2.2 concatenate.15
  123.0 15.8 %collective-permute-done.1.refs_4_ = bf16[16,128,512]{2,1,0:T(8,128)(2,1)} collective-permute-done((bf16[16,128,512]{2,1,0:T(8,128)(2,1)S(1)}, bf16[16,128,512]{2,1,0:T(8,128)(2,1)}, u32[]{:S(2)}, u32[]{:S(2)}) %collective-permute-start.1) | collective-permute-done | bytes 2097184 | tf_op jit(solution)/shard_map/ppermute | solution.py:246
  144.3 20.0 %collective-permute-done.3.refs_0_ = bf16[288,2176]{1,0:T(8,128)(2,1)} collective-permute-done((bf16[288,2176]{1,0:T(8,128)(2,1)S(1)}, bf16[288,2176]{1,0:T(8,128)(2,1)}, u32[]{:S(2)}, u32[]{:S(2)}) %collective-permute-start.3) | collective-permute-done | bytes 1253408 | tf_op jit(solution)/shard_map/ppermute | solution.py:310
  164.3 12.9 %collective-permute-start.4 = (bf16[288,2176]{1,0:T(8,128)(2,1)}, bf16[288,2176]{1,0:T(8,128)(2,1)S(1)}, u32[]{:S(2)}, u32[]{:S(2)}) collective-permute-start(bf16[288,2176]{1,0:T(8,128)(2,1)} %collective-permute-done.3.refs_0_), channel_id=1, source_target_pairs={{0,4},{1,3},{4,8},{5,1},{8,12},{9,5},{12,14},{13,9},{14,10},{15,13... | collective-permute-start | bytes 3760136 | tf_op jit(solution)/shard_map/ppermute | solution.py:310
  179.0 12.7 %collective-permute-done.5.refs_5_ = bf16[16,128,512]{2,1,0:T(8,128)(2,1)} collective-permute-done((bf16[16,128,512]{2,1,0:T(8,128)(2,1)}, bf16[16,128,512]{2,1,0:T(8,128)(2,1)}, u32[]{:S(2)}, u32[]{:S(2)}) %collective-permute-start.5) | collective-permute-done | bytes 2097184 | tf_op jit(solution)/shard_map/ppermute | solution.py:246
  192.1 2.8 collective-permute-start.6
  194.8 8.0 %expert_hidden.8 = (bf16[288,1024]{1,0:T(8,128)(2,1)S(1)}, bf16[288,1024]{1,0:T(8,128)(2,1)S(1)}) custom-call(s32[1]{0:T(128)} %bitcast.11.me_ref, bf16[288,2176]{1,0:T(8,128)(2,1)S(1)} %pad_maximum_fusion.refs_0_, bf16[288,2176]{1,0:T(8,128)(2,1)S(1)} %collective-permute-done.7.refs_1_, bf16[16,128,512]{2,1,0:T(8,128)(2,1)S(1)} %all-to-all-done.refs_2_, ...), custom_call_target="tpu_custom_call" | custom-call | flops 4831838208 | bytes 11927552 | tf_op jit(solution)/shard_map/expert_hidden/pallas_call | solution.py:133
  202.9 8.4 %expert_hidden.9 = (bf16[288,1024]{1,0:T(8,128)(2,1)S(1)}, bf16[288,1024]{1,0:T(8,128)(2,1)S(1)}) custom-call(s32[1]{0:T(128)} %bitcast.11.me_ref, bf16[288,2176]{1,0:T(8,128)(2,1)} %collective-permute-done.3.refs_0_, bf16[288,2176]{1,0:T(8,128)(2,1)S(1)} %collective-permute-done.8.refs_1_, bf16[16,128,512]{2,1,0:T(8,128)(2,1)S(1)} %all-to-all-done.refs_2_, ...), custom_call_target="tpu_custom_call" | custom-call | flops 4831838208 | bytes 11927552 | tf_op jit(solution)/shard_map/expert_hidden/pallas_call | solution.py:133
  211.4 24.0 %collective-permute-done.9.refs_3_ = bf16[16,128,512]{2,1,0:T(8,128)(2,1)S(1)} collective-permute-done((bf16[16,128,512]{2,1,0:T(8,128)(2,1)}, bf16[16,128,512]{2,1,0:T(8,128)(2,1)S(1)}, u32[]{:S(2)}, u32[]{:S(2)}) %collective-permute-start.9) | collective-permute-done | bytes 2097184 | tf_op jit(solution)/shard_map/ppermute | solution.py:246
  236.9 8.0 %expert_hidden.10 = (bf16[288,1024]{1,0:T(8,128)(2,1)S(1)}, bf16[288,1024]{1,0:T(8,128)(2,1)S(1)}) custom-call(s32[1]{0:T(128)} %bitcast.11.me_ref, bf16[288,2176]{1,0:T(8,128)(2,1)S(1)} %collective-permute-done.4.refs_0_, bf16[288,2176]{1,0:T(8,128)(2,1)S(1)} %collective-permute-done.12.refs_1_, bf16[16,128,512]{2,1,0:T(8,128)(2,1)S(1)} %all-to-all-done.refs_2_, ...), custom_call_target="tpu_custom_call" | custom-call | flops 4831838208 | bytes 11927552 | tf_op jit(solution)/shard_map/expert_hidden/pallas_call | solution.py:133
  244.9 7.6 %collective-permute-done.11.refs_0_ = bf16[288,2176]{1,0:T(8,128)(2,1)S(1)} collective-permute-done((bf16[288,2176]{1,0:T(8,128)(2,1)S(1)}, bf16[288,2176]{1,0:T(8,128)(2,1)S(1)}, u32[]{:S(2)}, u32[]{:S(2)}) %collective-permute-start.11) | collective-permute-done | bytes 1253408 | tf_op jit(solution)/shard_map/ppermute | solution.py:310
  252.6 8.1 %expert_hidden.11 = (bf16[288,1024]{1,0:T(8,128)(2,1)S(1)}, bf16[288,1024]{1,0:T(8,128)(2,1)S(1)}) custom-call(s32[1]{0:T(128)} %bitcast.11.me_ref, bf16[288,2176]{1,0:T(8,128)(2,1)S(1)} %collective-permute-done.6.refs_0_, bf16[288,2176]{1,0:T(8,128)(2,1)S(1)} %collective-permute-done.13.refs_1_, bf16[16,128,512]{2,1,0:T(8,128)(2,1)S(1)} %all-to-all-done.refs_2_, ...), custom_call_target="tpu_custom_call" | custom-call | flops 4831838208 | bytes 11927552 | tf_op jit(solution)/shard_map/expert_hidden/pallas_call | solution.py:133
  261.6 4.2 %expert_down.15 = (bf16[288,2048]{1,0:T(8,128)(2,1)S(1)}, bf16[288,2048]{1,0:T(8,128)(2,1)S(1)}) custom-call(bf16[288,1024]{1,0:T(8,128)(2,1)S(1)} %get-tuple-element.141.refs_0_, bf16[288,1024]{1,0:T(8,128)(2,1)S(1)} %get-tuple-element.142.refs_1_, bf16[16,128,512]{2,1,0:T(8,128)(2,1)} %all-to-all-done.2.refs_2_, ...), custom_call_target="tpu_custom_call" | custom-call | flops 2415919104 | bytes 7733248 | tf_op jit(solution)/shard_map/expert_down/pallas_call | solution.py:172
  267.1 8.0 %expert_hidden.12 = (bf16[288,1024]{1,0:T(8,128)(2,1)S(1)}, bf16[288,1024]{1,0:T(8,128)(2,1)S(1)}) custom-call(s32[1]{0:T(128)} %bitcast.11.me_ref, bf16[288,2176]{1,0:T(8,128)(2,1)S(1)} %collective-permute-done.11.refs_0_, bf16[288,2176]{1,0:T(8,128)(2,1)S(1)} %collective-permute-done.15.refs_1_, bf16[16,128,512]{2,1,0:T(8,128)(2,1)S(1)} %all-to-all-done.refs_2_, ...), custom_call_target="tpu_custom_call" | custom-call | flops 4831838208 | bytes 11927552 | tf_op jit(solution)/shard_map/expert_hidden/pallas_call | solution.py:133
  275.2 3.0 collective-permute-done.14.refs_0_
  278.6 4.2 %expert_down.14 = (bf16[288,2048]{1,0:T(8,128)(2,1)S(1)}, bf16[288,2048]{1,0:T(8,128)(2,1)S(1)}) custom-call(bf16[288,1024]{1,0:T(8,128)(2,1)S(1)} %get-tuple-element.137.refs_0_, bf16[288,1024]{1,0:T(8,128)(2,1)S(1)} %get-tuple-element.138.refs_1_, bf16[16,128,512]{2,1,0:T(8,128)(2,1)} %all-to-all-done.2.refs_2_, ...), custom_call_target="tpu_custom_call" | custom-call | flops 2415919104 | bytes 7733248 | tf_op jit(solution)/shard_map/expert_down/pallas_call | solution.py:172
  285.2 4.2 %expert_down.13 = (bf16[288,2048]{1,0:T(8,128)(2,1)S(1)}, bf16[288,2048]{1,0:T(8,128)(2,1)S(1)}) custom-call(bf16[288,1024]{1,0:T(8,128)(2,1)S(1)} %get-tuple-element.133.refs_0_, bf16[288,1024]{1,0:T(8,128)(2,1)S(1)} %get-tuple-element.134.refs_1_, bf16[16,128,512]{2,1,0:T(8,128)(2,1)} %all-to-all-done.2.refs_2_, ...), custom_call_target="tpu_custom_call" | custom-call | flops 2415919104 | bytes 7733248 | tf_op jit(solution)/shard_map/expert_down/pallas_call | solution.py:172
  290.1 8.1 %expert_hidden.13 = (bf16[288,1024]{1,0:T(8,128)(2,1)S(1)}, bf16[288,1024]{1,0:T(8,128)(2,1)S(1)}) custom-call(s32[1]{0:T(128)} %bitcast.11.me_ref, bf16[288,2176]{1,0:T(8,128)(2,1)S(1)} %collective-permute-done.14.refs_0_, bf16[288,2176]{1,0:T(8,128)(2,1)S(1)} %collective-permute-done.17.refs_1_, bf16[16,128,512]{2,1,0:T(8,128)(2,1)S(1)} %all-to-all-done.refs_2_, ...), custom_call_target="tpu_custom_call" | custom-call | flops 4831838208 | bytes 11927552 | tf_op jit(solution)/shard_map/expert_hidden/pallas_call | solution.py:133
  303.9 4.2 %expert_down.12 = (bf16[288,2048]{1,0:T(8,128)(2,1)S(1)}, bf16[288,2048]{1,0:T(8,128)(2,1)S(1)}) custom-call(bf16[288,1024]{1,0:T(8,128)(2,1)S(1)} %get-tuple-element.129.refs_0_, bf16[288,1024]{1,0:T(8,128)(2,1)S(1)} %get-tuple-element.130.refs_1_, bf16[16,128,512]{2,1,0:T(8,128)(2,1)} %all-to-all-done.2.refs_2_, ...), custom_call_target="tpu_custom_call" | custom-call | flops 2415919104 | bytes 7733248 | tf_op jit(solution)/shard_map/expert_down/pallas_call | solution.py:172
  309.9 4.7 %collective-permute-done.29.refs_2_ = bf16[288,1024]{1,0:T(8,128)(2,1)S(1)} collective-permute-done((bf16[288,1024]{1,0:T(8,128)(2,1)S(1)}, bf16[288,1024]{1,0:T(8,128)(2,1)S(1)}, u32[]{:S(2)}, u32[]{:S(2)}) %collective-permute-start.29) | collective-permute-done | bytes 589856 | tf_op jit(solution)/shard_map/ppermute | solution.py:342
  316.2 4.2 %expert_down.11 = (bf16[288,2048]{1,0:T(8,128)(2,1)S(1)}, bf16[288,2048]{1,0:T(8,128)(2,1)S(1)}) custom-call(bf16[288,1024]{1,0:T(8,128)(2,1)S(1)} %get-tuple-element.125.refs_0_, bf16[288,1024]{1,0:T(8,128)(2,1)S(1)} %get-tuple-element.126.refs_1_, bf16[16,128,512]{2,1,0:T(8,128)(2,1)} %all-to-all-done.2.refs_2_, ...), custom_call_target="tpu_custom_call" | custom-call | flops 2415919104 | bytes 7733248 | tf_op jit(solution)/shard_map/expert_down/pallas_call | solution.py:172
  320.6 8.1 %expert_hidden.14 = (bf16[288,1024]{1,0:T(8,128)(2,1)S(1)}, bf16[288,1024]{1,0:T(8,128)(2,1)S(1)}) custom-call(s32[1]{0:T(128)} %bitcast.11.me_ref, bf16[288,2176]{1,0:T(8,128)(2,1)S(1)} %collective-permute-done.16.refs_0_, bf16[288,2176]{1,0:T(8,128)(2,1)S(1)} %collective-permute-done.19.refs_1_, bf16[16,128,512]{2,1,0:T(8,128)(2,1)S(1)} %all-to-all-done.refs_2_, ...), custom_call_target="tpu_custom_call" | custom-call | flops 4831838208 | bytes 11927552 | tf_op jit(solution)/shard_map/expert_hidden/pallas_call | solution.py:133
  329.2 5.2 %collective-permute-done.36.refs_2_ = bf16[288,1024]{1,0:T(8,128)(2,1)S(1)} collective-permute-done((bf16[288,1024]{1,0:T(8,128)(2,1)S(1)}, bf16[288,1024]{1,0:T(8,128)(2,1)S(1)}, u32[]{:S(2)}, u32[]{:S(2)}) %collective-permute-start.36) | collective-permute-done | bytes 589856 | tf_op jit(solution)/shard_map/ppermute | solution.py:342
  335.8 4.9 %collective-permute-done.30.refs_2_ = bf16[288,1024]{1,0:T(8,128)(2,1)S(1)} collective-permute-done((bf16[288,1024]{1,0:T(8,128)(2,1)S(1)}, bf16[288,1024]{1,0:T(8,128)(2,1)S(1)}, u32[]{:S(2)}, u32[]{:S(2)}) %collective-permute-start.30) | collective-permute-done | bytes 589856 | tf_op jit(solution)/shard_map/ppermute | solution.py:342
  342.1 4.9 %collective-permute-done.37.refs_2_ = bf16[288,1024]{1,0:T(8,128)(2,1)S(1)} collective-permute-done((bf16[288,1024]{1,0:T(8,128)(2,1)S(1)}, bf16[288,1024]{1,0:T(8,128)(2,1)S(1)}, u32[]{:S(2)}, u32[]{:S(2)}) %collective-permute-start.37) | collective-permute-done | bytes 589856 | tf_op jit(solution)/shard_map/ppermute | solution.py:342
  348.4 4.9 %collective-permute-done.31.refs_2_ = bf16[288,1024]{1,0:T(8,128)(2,1)S(1)} collective-permute-done((bf16[288,1024]{1,0:T(8,128)(2,1)S(1)}, bf16[288,1024]{1,0:T(8,128)(2,1)S(1)}, u32[]{:S(2)}, u32[]{:S(2)}) %collective-permute-start.31) | collective-permute-done | bytes 589856 | tf_op jit(solution)/shard_map/ppermute | solution.py:342
  355.0 4.2 %expert_down.10 = (bf16[288,2048]{1,0:T(8,128)(2,1)S(1)}, bf16[288,2048]{1,0:T(8,128)(2,1)S(1)}) custom-call(bf16[288,1024]{1,0:T(8,128)(2,1)S(1)} %get-tuple-element.121.refs_0_, bf16[288,1024]{1,0:T(8,128)(2,1)S(1)} %get-tuple-element.122.refs_1_, bf16[16,128,512]{2,1,0:T(8,128)(2,1)} %all-to-all-done.2.refs_2_, ...), custom_call_target="tpu_custom_call" | custom-call | flops 2415919104 | bytes 7733248 | tf_op jit(solution)/shard_map/expert_down/pallas_call | solution.py:172
  359.3 8.0 %expert_hidden.15 = (bf16[288,1024]{1,0:T(8,128)(2,1)S(1)}, bf16[288,1024]{1,0:T(8,128)(2,1)S(1)}) custom-call(s32[1]{0:T(128)} %bitcast.11.me_ref, bf16[288,2176]{1,0:T(8,128)(2,1)S(1)} %collective-permute-done.18.refs_0_, bf16[288,2176]{1,0:T(8,128)(2,1)S(1)} %collective-permute-done.20.refs_1_, bf16[16,128,512]{2,1,0:T(8,128)(2,1)S(1)} %all-to-all-done.refs_2_, ...), custom_call_target="tpu_custom_call" | custom-call | flops 4831838208 | bytes 11927552 | tf_op jit(solution)/shard_map/expert_hidden/pallas_call | solution.py:133
  367.4 4.2 %expert_down.9 = (bf16[288,2048]{1,0:T(8,128)(2,1)S(1)}, bf16[288,2048]{1,0:T(8,128)(2,1)S(1)}) custom-call(bf16[288,1024]{1,0:T(8,128)(2,1)S(1)} %get-tuple-element.117.refs_0_, bf16[288,1024]{1,0:T(8,128)(2,1)S(1)} %get-tuple-element.118.refs_1_, bf16[16,128,512]{2,1,0:T(8,128)(2,1)} %all-to-all-done.2.refs_2_, ...), custom_call_target="tpu_custom_call" | custom-call | flops 2415919104 | bytes 7733248 | tf_op jit(solution)/shard_map/expert_down/pallas_call | solution.py:172
  373.9 4.2 %expert_down.8 = (bf16[288,2048]{1,0:T(8,128)(2,1)S(1)}, bf16[288,2048]{1,0:T(8,128)(2,1)S(1)}) custom-call(bf16[288,1024]{1,0:T(8,128)(2,1)S(1)} %get-tuple-element.91.refs_0_, bf16[288,1024]{1,0:T(8,128)(2,1)S(1)} %get-tuple-element.92.refs_1_, bf16[16,128,512]{2,1,0:T(8,128)(2,1)} %all-to-all-done.2.refs_2_, ...), custom_call_target="tpu_custom_call" | custom-call | flops 2415919104 | bytes 7733248 | tf_op jit(solution)/shard_map/expert_down/pallas_call | solution.py:172
  379.9 2.4 collective-permute-done.39.refs_2_
  384.0 4.6 %collective-permute-done.33.refs_2_ = bf16[288,1024]{1,0:T(8,128)(2,1)S(1)} collective-permute-done((bf16[288,1024]{1,0:T(8,128)(2,1)S(1)}, bf16[288,1024]{1,0:T(8,128)(2,1)S(1)}, u32[]{:S(2)}, u32[]{:S(2)}) %collective-permute-start.33) | collective-permute-done | bytes 589856 | tf_op jit(solution)/shard_map/ppermute | solution.py:342
  390.4 4.6 %collective-permute-done.40.refs_2_ = bf16[288,1024]{1,0:T(8,128)(2,1)S(1)} collective-permute-done((bf16[288,1024]{1,0:T(8,128)(2,1)S(1)}, bf16[288,1024]{1,0:T(8,128)(2,1)S(1)}, u32[]{:S(2)}, u32[]{:S(2)}) %collective-permute-start.40) | collective-permute-done | bytes 589856 | tf_op jit(solution)/shard_map/ppermute | solution.py:342
  396.7 4.6 %collective-permute-done.34.refs_2_ = bf16[288,1024]{1,0:T(8,128)(2,1)S(1)} collective-permute-done((bf16[288,1024]{1,0:T(8,128)(2,1)S(1)}, bf16[288,1024]{1,0:T(8,128)(2,1)S(1)}, u32[]{:S(2)}, u32[]{:S(2)}) %collective-permute-start.34) | collective-permute-done | bytes 589856 | tf_op jit(solution)/shard_map/ppermute | solution.py:342
  401.5 6.1 %collective-permute-done.41.refs_2_ = bf16[288,1024]{1,0:T(8,128)(2,1)S(1)} collective-permute-done((bf16[288,1024]{1,0:T(8,128)(2,1)S(1)}, bf16[288,1024]{1,0:T(8,128)(2,1)S(1)}, u32[]{:S(2)}, u32[]{:S(2)}) %collective-permute-start.41) | collective-permute-done | bytes 589856 | tf_op jit(solution)/shard_map/ppermute | solution.py:342
  410.0 3.2 fusion.2
  (118 shorter events, 50.9 us)
Async XLA Ops:
  3.8 48.5 %all-to-all-start = ((bf16[16,128,512]{2,1,0:T(8,128)(2,1)}), bf16[16,128,512]{2,1,0:T(8,128)(2,1)S(1)}, u32[]{:S(2)}, u32[]{:S(2)}) async-start(bf16[16,128,512]{2,1,0:T(8,128)(2,1)} %fusion), calls=%async_computation | async-start | bytes 4194304 | tf_op jit(solution)/shard_map/all_to_all | solution.py:242
  11.2 6.4 %copy-start.1 = (bf16[1,576,2048]{2,1,0:T(8,128)(2,1)S(1)}, bf16[1,576,2048]{2,1,0:T(8,128)(2,1)}, u32[]{:S(2)}) copy-start(bf16[1,576,2048]{2,1,0:T(8,128)(2,1)} %param.10) | copy-start | bytes 7077892
  52.3 52.4 %all-to-all-start.1 = ((bf16[16,128,512]{2,1,0:T(8,128)(2,1)}), bf16[16,128,512]{2,1,0:T(8,128)(2,1)}, u32[]{:S(2)}, u32[]{:S(2)}) async-start(bf16[16,128,512]{2,1,0:T(8,128)(2,1)} %get-tuple-element.78), calls=%async_computation.1 | async-start | bytes 4194304 | tf_op jit(solution)/shard_map/all_to_all | solution.py:242
  65.4 29.0 %collective-permute-start = (bf16[288,2048]{1,0:T(8,128)(2,1)S(1)}, bf16[288,2048]{1,0:T(8,128)(2,1)}, u32[]{:S(2)}, u32[]{:S(2)}) collective-permute-start(bf16[288,2048]{1,0:T(8,128)(2,1)S(1)} %fusion.1), channel_id=1, source_target_pairs={{0,16},{16,0},{1,17},{17,1},{2,18},{18,2},{3,19},{19,3},{4,20},{20... | collective-permute-start | bytes 3538952 | tf_op jit(solution)/shard_map/ppermute | solution.py:276
  67.0 71.8 %collective-permute-start.1 = (bf16[16,128,512]{2,1,0:T(8,128)(2,1)S(1)}, bf16[16,128,512]{2,1,0:T(8,128)(2,1)}, u32[]{:S(2)}, u32[]{:S(2)}) collective-permute-start(bf16[16,128,512]{2,1,0:T(8,128)(2,1)S(1)} %all-to-all-done.refs_2_), channel_id=1, source_target_pairs={{0,16},{16,0},{1,17},{17,1},{2,18},{18,2},{3,19},{19,3},{4,20},{20... | collective-permute-start | bytes 6291464 | tf_op jit(solution)/shard_map/ppermute | solution.py:246
  98.7 17.3 %copy-start.8 = (s32[1,288,8]{1,2,0:T(8,128)S(1)}, s32[1,288,8]{1,2,0:T(8,128)}, u32[]{:S(2)}) copy-start(s32[1,288,8]{1,2,0:T(8,128)} %param.18) | copy-start | bytes 27652
  104.7 59.6 %all-to-all-start.2 = ((bf16[16,128,512]{2,1,0:T(8,128)(2,1)}), bf16[16,128,512]{2,1,0:T(8,128)(2,1)}, u32[]{:S(2)}, u32[]{:S(2)}) async-start(bf16[16,128,512]{2,1,0:T(8,128)(2,1)} %get-tuple-element.83), calls=%async_computation.2 | async-start | bytes 4194304 | tf_op jit(solution)/shard_map/all_to_all | solution.py:242
  138.9 2.1 collective-permute-start.2
  141.1 23.2 %collective-permute-start.3 = (bf16[288,2176]{1,0:T(8,128)(2,1)S(1)}, bf16[288,2176]{1,0:T(8,128)(2,1)}, u32[]{:S(2)}, u32[]{:S(2)}) collective-permute-start(bf16[288,2176]{1,0:T(8,128)(2,1)S(1)} %pad_maximum_fusion.refs_0_), channel_id=1, source_target_pairs={{0,4},{1,3},{4,8},{5,1},{8,12},{9,5},{12,14},{13,9},{14,10},{15,13... | collective-permute-start | bytes 3760136 | tf_op jit(solution)/shard_map/ppermute | solution.py:310
  142.8 48.8 %collective-permute-start.5 = (bf16[16,128,512]{2,1,0:T(8,128)(2,1)}, bf16[16,128,512]{2,1,0:T(8,128)(2,1)}, u32[]{:S(2)}, u32[]{:S(2)}) collective-permute-start(bf16[16,128,512]{2,1,0:T(8,128)(2,1)} %all-to-all-done.1.refs_3_), channel_id=1, source_target_pairs={{0,16},{16,0},{1,17},{17,1},{2,18},{18,2},{3,19},{19,3},{4,20},{20... | collective-permute-start | bytes 6291464 | tf_op jit(solution)/shard_map/ppermute | solution.py:246
  164.3 27.8 %collective-permute-start.4 = (bf16[288,2176]{1,0:T(8,128)(2,1)}, bf16[288,2176]{1,0:T(8,128)(2,1)S(1)}, u32[]{:S(2)}, u32[]{:S(2)}) collective-permute-start(bf16[288,2176]{1,0:T(8,128)(2,1)} %collective-permute-done.3.refs_0_), channel_id=1, source_target_pairs={{0,4},{1,3},{4,8},{5,1},{8,12},{9,5},{12,14},{13,9},{14,10},{15,13... | collective-permute-start | bytes 3760136 | tf_op jit(solution)/shard_map/ppermute | solution.py:310
  177.2 17.6 %collective-permute-start.7 = (bf16[288,2176]{1,0:T(8,128)(2,1)S(1)}, bf16[288,2176]{1,0:T(8,128)(2,1)S(1)}, u32[]{:S(2)}, u32[]{:S(2)}) collective-permute-start(bf16[288,2176]{1,0:T(8,128)(2,1)S(1)} %pad_maximum_fusion.refs_0_), channel_id=1, source_target_pairs={{0,1},{1,0},{2,3},{3,2},{4,5},{5,4},{6,7},{7,6},{8,9},{9,8},{10,11... | collective-permute-start | bytes 3760136 | tf_op jit(solution)/shard_map/ppermute | solution.py:306
  177.2 58.1 %collective-permute-start.9 = (bf16[16,128,512]{2,1,0:T(8,128)(2,1)}, bf16[16,128,512]{2,1,0:T(8,128)(2,1)S(1)}, u32[]{:S(2)}, u32[]{:S(2)}) collective-permute-start(bf16[16,128,512]{2,1,0:T(8,128)(2,1)} %all-to-all-done.2.refs_2_), channel_id=1, source_target_pairs={{0,16},{16,0},{1,17},{17,1},{2,18},{18,2},{3,19},{19,3},{4,20},{20... | collective-permute-start | bytes 6291464 | tf_op jit(solution)/shard_map/ppermute | solution.py:246
  178.8 24.1 %collective-permute-start.8 = (bf16[288,2176]{1,0:T(8,128)(2,1)}, bf16[288,2176]{1,0:T(8,128)(2,1)S(1)}, u32[]{:S(2)}, u32[]{:S(2)}) collective-permute-start(bf16[288,2176]{1,0:T(8,128)(2,1)} %collective-permute-done.3.refs_0_), channel_id=1, source_target_pairs={{0,1},{1,0},{2,3},{3,2},{4,5},{5,4},{6,7},{7,6},{8,9},{9,8},{10,11... | collective-permute-start | bytes 3760136 | tf_op jit(solution)/shard_map/ppermute | solution.py:306
  192.1 19.3 %collective-permute-start.6 = (bf16[288,2176]{1,0:T(8,128)(2,1)S(1)}, bf16[288,2176]{1,0:T(8,128)(2,1)S(1)}, u32[]{:S(2)}, u32[]{:S(2)}) collective-permute-start(bf16[288,2176]{1,0:T(8,128)(2,1)S(1)} %collective-permute-done.4.refs_0_), channel_id=1, source_target_pairs={{0,4},{1,3},{4,8},{5,1},{8,12},{9,5},{12,14},{13,9},{14,10},{15,13... | collective-permute-start | bytes 3760136 | tf_op jit(solution)/shard_map/ppermute | solution.py:310
  194.8 42.0 %collective-permute-start.12 = (bf16[288,2176]{1,0:T(8,128)(2,1)S(1)}, bf16[288,2176]{1,0:T(8,128)(2,1)S(1)}, u32[]{:S(2)}, u32[]{:S(2)}) collective-permute-start(bf16[288,2176]{1,0:T(8,128)(2,1)S(1)} %collective-permute-done.4.refs_0_), channel_id=1, source_target_pairs={{0,1},{1,0},{2,3},{3,2},{4,5},{5,4},{6,7},{7,6},{8,9},{9,8},{10,11... | collective-permute-start | bytes 3760136 | tf_op jit(solution)/shard_map/ppermute | solution.py:306
  235.3 17.2 %collective-permute-start.11 = (bf16[288,2176]{1,0:T(8,128)(2,1)S(1)}, bf16[288,2176]{1,0:T(8,128)(2,1)S(1)}, u32[]{:S(2)}, u32[]{:S(2)}) collective-permute-start(bf16[288,2176]{1,0:T(8,128)(2,1)S(1)} %collective-permute-done.6.refs_0_), channel_id=1, source_target_pairs={{0,4},{1,3},{4,8},{5,1},{8,12},{9,5},{12,14},{13,9},{14,10},{15,13... | collective-permute-start | bytes 3760136 | tf_op jit(solution)/shard_map/ppermute | solution.py:310
  235.9 16.6 %collective-permute-start.13 = (bf16[288,2176]{1,0:T(8,128)(2,1)S(1)}, bf16[288,2176]{1,0:T(8,128)(2,1)S(1)}, u32[]{:S(2)}, u32[]{:S(2)}) collective-permute-start(bf16[288,2176]{1,0:T(8,128)(2,1)S(1)} %collective-permute-done.6.refs_0_), channel_id=1, source_target_pairs={{0,1},{1,0},{2,3},{3,2},{4,5},{5,4},{6,7},{7,6},{8,9},{9,8},{10,11... | collective-permute-start | bytes 3760136 | tf_op jit(solution)/shard_map/ppermute | solution.py:306
  260.6 6.5 %collective-permute-start.15 = (bf16[288,2176]{1,0:T(8,128)(2,1)S(1)}, bf16[288,2176]{1,0:T(8,128)(2,1)S(1)}, u32[]{:S(2)}, u32[]{:S(2)}) collective-permute-start(bf16[288,2176]{1,0:T(8,128)(2,1)S(1)} %collective-permute-done.11.refs_0_), channel_id=1, source_target_pairs={{0,1},{1,0},{2,3},{3,2},{4,5},{5,4},{6,7},{7,6},{8,9},{9,8},{10,11... | collective-permute-start | bytes 3760136 | tf_op jit(solution)/shard_map/ppermute | solution.py:306
  260.7 17.5 %collective-permute-start.14 = (bf16[288,2176]{1,0:T(8,128)(2,1)S(1)}, bf16[288,2176]{1,0:T(8,128)(2,1)S(1)}, u32[]{:S(2)}, u32[]{:S(2)}) collective-permute-start(bf16[288,2176]{1,0:T(8,128)(2,1)S(1)} %collective-permute-done.11.refs_0_), channel_id=1, source_target_pairs={{0,4},{1,3},{4,8},{5,1},{8,12},{9,5},{12,14},{13,9},{14,10},{15,13... | collective-permute-start | bytes 3760136 | tf_op jit(solution)/shard_map/ppermute | solution.py:310
  265.8 18.4 %collective-permute-start.27 = (bf16[288,2048]{1,0:T(8,128)(2,1)S(1)}, bf16[288,2048]{1,0:T(8,128)(2,1)S(1)}, u32[]{:S(2)}, u32[]{:S(2)}) collective-permute-start(bf16[288,2048]{1,0:T(8,128)(2,1)S(1)} %get-tuple-element.144), channel_id=1, source_target_pairs={{0,1},{1,0},{2,3},{3,2},{4,5},{5,4},{6,7},{7,6},{8,9},{9,8},{10,11... | collective-permute-start | bytes 3538952 | tf_op jit(solution)/shard_map/ppermute | solution.py:333
  278.2 11.9 %collective-permute-start.17 = (bf16[288,2176]{1,0:T(8,128)(2,1)S(1)}, bf16[288,2176]{1,0:T(8,128)(2,1)S(1)}, u32[]{:S(2)}, u32[]{:S(2)}) collective-permute-start(bf16[288,2176]{1,0:T(8,128)(2,1)S(1)} %collective-permute-done.14.refs_0_), channel_id=1, source_target_pairs={{0,1},{1,0},{2,3},{3,2},{4,5},{5,4},{6,7},{7,6},{8,9},{9,8},{10,11... | collective-permute-start | bytes 3760136 | tf_op jit(solution)/shard_map/ppermute | solution.py:306
  278.2 19.9 %collective-permute-start.16 = (bf16[288,2176]{1,0:T(8,128)(2,1)S(1)}, bf16[288,2176]{1,0:T(8,128)(2,1)S(1)}, u32[]{:S(2)}, u32[]{:S(2)}) collective-permute-start(bf16[288,2176]{1,0:T(8,128)(2,1)S(1)} %collective-permute-done.14.refs_0_), channel_id=1, source_target_pairs={{0,4},{1,3},{4,8},{5,1},{8,12},{9,5},{12,14},{13,9},{14,10},{15,13... | collective-permute-start | bytes 3760136 | tf_op jit(solution)/shard_map/ppermute | solution.py:310
  282.8 18.7 %collective-permute-start.26 = (bf16[288,2048]{1,0:T(8,128)(2,1)S(1)}, bf16[288,2048]{1,0:T(8,128)(2,1)S(1)}, u32[]{:S(2)}, u32[]{:S(2)}) collective-permute-start(bf16[288,2048]{1,0:T(8,128)(2,1)S(1)} %get-tuple-element.140), channel_id=1, source_target_pairs={{0,1},{1,0},{2,3},{3,2},{4,5},{5,4},{6,7},{7,6},{8,9},{9,8},{10,11... | collective-permute-start | bytes 3538952 | tf_op jit(solution)/shard_map/ppermute | solution.py:333
  284.4 17.2 %collective-permute-start.28 = (bf16[288,1024]{1,0:T(8,128)(2,1)S(1)}, bf16[288,1024]{1,0:T(8,128)(2,1)S(1)}, u32[]{:S(2)}, u32[]{:S(2)}) collective-permute-start(bf16[288,1024]{1,0:T(8,128)(2,1)S(1)} %add_terms.16), channel_id=1, source_target_pairs={{0,4},{1,3},{4,8},{5,1},{8,12},{9,5},{12,14},{13,9},{14,10},{15,13... | collective-permute-start | bytes 1769480 | tf_op jit(solution)/shard_map/ppermute | solution.py:342
  289.4 19.2 %collective-permute-start.25 = (bf16[288,2048]{1,0:T(8,128)(2,1)S(1)}, bf16[288,2048]{1,0:T(8,128)(2,1)S(1)}, u32[]{:S(2)}, u32[]{:S(2)}) collective-permute-start(bf16[288,2048]{1,0:T(8,128)(2,1)S(1)} %get-tuple-element.136), channel_id=1, source_target_pairs={{0,1},{1,0},{2,3},{3,2},{4,5},{5,4},{6,7},{7,6},{8,9},{9,8},{10,11... | collective-permute-start | bytes 3538952 | tf_op jit(solution)/shard_map/ppermute | solution.py:333
  298.2 22.3 %collective-permute-start.19 = (bf16[288,2176]{1,0:T(8,128)(2,1)S(1)}, bf16[288,2176]{1,0:T(8,128)(2,1)S(1)}, u32[]{:S(2)}, u32[]{:S(2)}) collective-permute-start(bf16[288,2176]{1,0:T(8,128)(2,1)S(1)} %collective-permute-done.16.refs_0_), channel_id=1, source_target_pairs={{0,1},{1,0},{2,3},{3,2},{4,5},{5,4},{6,7},{7,6},{8,9},{9,8},{10,11... | collective-permute-start | bytes 3760136 | tf_op jit(solution)/shard_map/ppermute | solution.py:306
  298.4 9.9 %collective-permute-start.35 = (bf16[288,1024]{1,0:T(8,128)(2,1)S(1)}, bf16[288,1024]{1,0:T(8,128)(2,1)S(1)}, u32[]{:S(2)}, u32[]{:S(2)}) collective-permute-start(bf16[288,1024]{1,0:T(8,128)(2,1)S(1)} %add_terms.24), channel_id=1, source_target_pairs={{0,4},{1,3},{4,8},{5,1},{8,12},{9,5},{12,14},{13,9},{14,10},{15,13... | collective-permute-start | bytes 1769480 | tf_op jit(solution)/shard_map/ppermute | solution.py:342
  301.8 12.9 %collective-permute-start.29 = (bf16[288,1024]{1,0:T(8,128)(2,1)S(1)}, bf16[288,1024]{1,0:T(8,128)(2,1)S(1)}, u32[]{:S(2)}, u32[]{:S(2)}) collective-permute-start(bf16[288,1024]{1,0:T(8,128)(2,1)S(1)} %add_terms.17), channel_id=1, source_target_pairs={{0,4},{1,3},{4,8},{5,1},{8,12},{9,5},{12,14},{13,9},{14,10},{15,13... | collective-permute-start | bytes 1769480 | tf_op jit(solution)/shard_map/ppermute | solution.py:342
  302.2 26.4 %collective-permute-start.18 = (bf16[288,2176]{1,0:T(8,128)(2,1)S(1)}, bf16[288,2176]{1,0:T(8,128)(2,1)S(1)}, u32[]{:S(2)}, u32[]{:S(2)}) collective-permute-start(bf16[288,2176]{1,0:T(8,128)(2,1)S(1)} %collective-permute-done.16.refs_0_), channel_id=1, source_target_pairs={{0,4},{1,3},{4,8},{5,1},{8,12},{9,5},{12,14},{13,9},{14,10},{15,13... | collective-permute-start | bytes 3760136 | tf_op jit(solution)/shard_map/ppermute | solution.py:310
  308.3 32.4 %collective-permute-start.24 = (bf16[288,2048]{1,0:T(8,128)(2,1)S(1)}, bf16[288,2048]{1,0:T(8,128)(2,1)S(1)}, u32[]{:S(2)}, u32[]{:S(2)}) collective-permute-start(bf16[288,2048]{1,0:T(8,128)(2,1)S(1)} %get-tuple-element.132), channel_id=1, source_target_pairs={{0,1},{1,0},{2,3},{3,2},{4,5},{5,4},{6,7},{7,6},{8,9},{9,8},{10,11... | collective-permute-start | bytes 3538952 | tf_op jit(solution)/shard_map/ppermute | solution.py:333
  308.6 25.8 %collective-permute-start.36 = (bf16[288,1024]{1,0:T(8,128)(2,1)S(1)}, bf16[288,1024]{1,0:T(8,128)(2,1)S(1)}, u32[]{:S(2)}, u32[]{:S(2)}) collective-permute-start(bf16[288,1024]{1,0:T(8,128)(2,1)S(1)} %add_terms.25), channel_id=1, source_target_pairs={{0,4},{1,3},{4,8},{5,1},{8,12},{9,5},{12,14},{13,9},{14,10},{15,13... | collective-permute-start | bytes 1769480 | tf_op jit(solution)/shard_map/ppermute | solution.py:342
  314.9 25.9 %collective-permute-start.30 = (bf16[288,1024]{1,0:T(8,128)(2,1)S(1)}, bf16[288,1024]{1,0:T(8,128)(2,1)S(1)}, u32[]{:S(2)}, u32[]{:S(2)}) collective-permute-start(bf16[288,1024]{1,0:T(8,128)(2,1)S(1)} %add_terms.18), channel_id=1, source_target_pairs={{0,4},{1,3},{4,8},{5,1},{8,12},{9,5},{12,14},{13,9},{14,10},{15,13... | collective-permute-start | bytes 1769480 | tf_op jit(solution)/shard_map/ppermute | solution.py:342
  320.5 32.9 %collective-permute-start.23 = (bf16[288,2048]{1,0:T(8,128)(2,1)S(1)}, bf16[288,2048]{1,0:T(8,128)(2,1)S(1)}, u32[]{:S(2)}, u32[]{:S(2)}) collective-permute-start(bf16[288,2048]{1,0:T(8,128)(2,1)S(1)} %get-tuple-element.128), channel_id=1, source_target_pairs={{0,1},{1,0},{2,3},{3,2},{4,5},{5,4},{6,7},{7,6},{8,9},{9,8},{10,11... | collective-permute-start | bytes 3538952 | tf_op jit(solution)/shard_map/ppermute | solution.py:333
  328.6 30.7 %collective-permute-start.20 = (bf16[288,2176]{1,0:T(8,128)(2,1)S(1)}, bf16[288,2176]{1,0:T(8,128)(2,1)S(1)}, u32[]{:S(2)}, u32[]{:S(2)}) collective-permute-start(bf16[288,2176]{1,0:T(8,128)(2,1)S(1)} %collective-permute-done.18.refs_0_), channel_id=1, source_target_pairs={{0,1},{1,0},{2,3},{3,2},{4,5},{5,4},{6,7},{7,6},{8,9},{9,8},{10,11... | collective-permute-start | bytes 3760136 | tf_op jit(solution)/shard_map/ppermute | solution.py:306
  334.6 12.4 %collective-permute-start.37 = (bf16[288,1024]{1,0:T(8,128)(2,1)S(1)}, bf16[288,1024]{1,0:T(8,128)(2,1)S(1)}, u32[]{:S(2)}, u32[]{:S(2)}) collective-permute-start(bf16[288,1024]{1,0:T(8,128)(2,1)S(1)} %add_terms.26), channel_id=1, source_target_pairs={{0,4},{1,3},{4,8},{5,1},{8,12},{9,5},{12,14},{13,9},{14,10},{15,13... | collective-permute-start | bytes 1769480 | tf_op jit(solution)/shard_map/ppermute | solution.py:342
  340.9 12.4 %collective-permute-start.31 = (bf16[288,1024]{1,0:T(8,128)(2,1)S(1)}, bf16[288,1024]{1,0:T(8,128)(2,1)S(1)}, u32[]{:S(2)}, u32[]{:S(2)}) collective-permute-start(bf16[288,1024]{1,0:T(8,128)(2,1)S(1)} %add_terms.19), channel_id=1, source_target_pairs={{0,4},{1,3},{4,8},{5,1},{8,12},{9,5},{12,14},{13,9},{14,10},{15,13... | collective-permute-start | bytes 1769480 | tf_op jit(solution)/shard_map/ppermute | solution.py:342
  347.3 24.9 %collective-permute-start.38 = (bf16[288,1024]{1,0:T(8,128)(2,1)S(1)}, bf16[288,1024]{1,0:T(8,128)(2,1)S(1)}, u32[]{:S(2)}, u32[]{:S(2)}) collective-permute-start(bf16[288,1024]{1,0:T(8,128)(2,1)S(1)} %add_terms.27), channel_id=1, source_target_pairs={{0,4},{1,3},{4,8},{5,1},{8,12},{9,5},{12,14},{13,9},{14,10},{15,13... | collective-permute-start | bytes 1769480 | tf_op jit(solution)/shard_map/ppermute | solution.py:342
  353.6 24.5 %collective-permute-start.32 = (bf16[288,1024]{1,0:T(8,128)(2,1)S(1)}, bf16[288,1024]{1,0:T(8,128)(2,1)S(1)}, u32[]{:S(2)}, u32[]{:S(2)}) collective-permute-start(bf16[288,1024]{1,0:T(8,128)(2,1)S(1)} %add_terms.20), channel_id=1, source_target_pairs={{0,4},{1,3},{4,8},{5,1},{8,12},{9,5},{12,14},{13,9},{14,10},{15,13... | collective-permute-start | bytes 1769480 | tf_op jit(solution)/shard_map/ppermute | solution.py:342
  359.2 18.9 %collective-permute-start.22 = (bf16[288,2048]{1,0:T(8,128)(2,1)S(1)}, bf16[288,2048]{1,0:T(8,128)(2,1)S(1)}, u32[]{:S(2)}, u32[]{:S(2)}) collective-permute-start(bf16[288,2048]{1,0:T(8,128)(2,1)S(1)} %get-tuple-element.124), channel_id=1, source_target_pairs={{0,1},{1,0},{2,3},{3,2},{4,5},{5,4},{6,7},{7,6},{8,9},{9,8},{10,11... | collective-permute-start | bytes 3538952 | tf_op jit(solution)/shard_map/ppermute | solution.py:333
  371.6 17.0 %collective-permute-start.21 = (bf16[288,2048]{1,0:T(8,128)(2,1)S(1)}, bf16[288,2048]{1,0:T(8,128)(2,1)S(1)}, u32[]{:S(2)}, u32[]{:S(2)}) collective-permute-start(bf16[288,2048]{1,0:T(8,128)(2,1)S(1)} %get-tuple-element.120), channel_id=1, source_target_pairs={{0,1},{1,0},{2,3},{3,2},{4,5},{5,4},{6,7},{7,6},{8,9},{9,8},{10,11... | collective-permute-start | bytes 3538952 | tf_op jit(solution)/shard_map/ppermute | solution.py:333
  372.4 9.9 %collective-permute-start.39 = (bf16[288,1024]{1,0:T(8,128)(2,1)S(1)}, bf16[288,1024]{1,0:T(8,128)(2,1)S(1)}, u32[]{:S(2)}, u32[]{:S(2)}) collective-permute-start(bf16[288,1024]{1,0:T(8,128)(2,1)S(1)} %add_terms.28), channel_id=1, source_target_pairs={{0,4},{1,3},{4,8},{5,1},{8,12},{9,5},{12,14},{13,9},{14,10},{15,13... | collective-permute-start | bytes 1769480 | tf_op jit(solution)/shard_map/ppermute | solution.py:342
  378.4 10.3 %collective-permute-start.33 = (bf16[288,1024]{1,0:T(8,128)(2,1)S(1)}, bf16[288,1024]{1,0:T(8,128)(2,1)S(1)}, u32[]{:S(2)}, u32[]{:S(2)}) collective-permute-start(bf16[288,1024]{1,0:T(8,128)(2,1)S(1)} %add_terms.21), channel_id=1, source_target_pairs={{0,4},{1,3},{4,8},{5,1},{8,12},{9,5},{12,14},{13,9},{14,10},{15,13... | collective-permute-start | bytes 1769480 | tf_op jit(solution)/shard_map/ppermute | solution.py:342
  379.9 16.8 %collective-permute-start.10 = (bf16[288,2048]{1,0:T(8,128)(2,1)S(1)}, bf16[288,2048]{1,0:T(8,128)(2,1)S(1)}, u32[]{:S(2)}, u32[]{:S(2)}) collective-permute-start(bf16[288,2048]{1,0:T(8,128)(2,1)S(1)} %get-tuple-element.100), channel_id=1, source_target_pairs={{0,1},{1,0},{2,3},{3,2},{4,5},{5,4},{6,7},{7,6},{8,9},{9,8},{10,11... | collective-permute-start | bytes 3538952 | tf_op jit(solution)/shard_map/ppermute | solution.py:333
  382.5 12.4 %collective-permute-start.40 = (bf16[288,1024]{1,0:T(8,128)(2,1)S(1)}, bf16[288,1024]{1,0:T(8,128)(2,1)S(1)}, u32[]{:S(2)}, u32[]{:S(2)}) collective-permute-start(bf16[288,1024]{1,0:T(8,128)(2,1)S(1)} %add_terms.29), channel_id=1, source_target_pairs={{0,4},{1,3},{4,8},{5,1},{8,12},{9,5},{12,14},{13,9},{14,10},{15,13... | collective-permute-start | bytes 1769480 | tf_op jit(solution)/shard_map/ppermute | solution.py:342
  388.8 12.4 %collective-permute-start.34 = (bf16[288,1024]{1,0:T(8,128)(2,1)S(1)}, bf16[288,1024]{1,0:T(8,128)(2,1)S(1)}, u32[]{:S(2)}, u32[]{:S(2)}) collective-permute-start(bf16[288,1024]{1,0:T(8,128)(2,1)S(1)} %add_terms.22), channel_id=1, source_target_pairs={{0,4},{1,3},{4,8},{5,1},{8,12},{9,5},{12,14},{13,9},{14,10},{15,13... | collective-permute-start | bytes 1769480 | tf_op jit(solution)/shard_map/ppermute | solution.py:342
  395.2 12.4 %collective-permute-start.41 = (bf16[288,1024]{1,0:T(8,128)(2,1)S(1)}, bf16[288,1024]{1,0:T(8,128)(2,1)S(1)}, u32[]{:S(2)}, u32[]{:S(2)}) collective-permute-start(bf16[288,1024]{1,0:T(8,128)(2,1)S(1)} %add_terms.30), channel_id=1, source_target_pairs={{0,4},{1,3},{4,8},{5,1},{8,12},{9,5},{12,14},{13,9},{14,10},{15,13... | collective-permute-start | bytes 1769480 | tf_op jit(solution)/shard_map/ppermute | solution.py:342
  407.9 2.1 collective-permute-start.42
  (8 other events, 32.9 us)
where the time goes:
time: 421 us; the launch traced here: 414 us
  waiting for transfers between devices  176 us (42%)
  Pallas kernels  126 us (30%)
  starting transfers between devices  79.6 us (19%)
  local copies, waits for them, and re-layouts  19.3 us (5%)
  other arithmetic  11.8 us (3%)
    pallas_call x8, Pallas kernels, expert_hidden(): pl.pallas_call(functools.partial(hidden_kernel, experts, width), in_specs...  64.8 us
    ppermute x3, waiting for transfers between devices, over_kv(): lax.ppermute(part, 'kv', [(i, (i + turn) % kv) for i in range(kv)])  52.4 us
    ppermute x14, waiting for transfers between devices, on_device(): running = lax.ppermute(running, 'ex', ring)  49.3 us
    pallas_call x8, Pallas kernels, expert_down(): pl.pallas_call(down_kernel, in_specs=[vmem] * (2 + len(weights)), out_spe...  33.8 us
    ppermute x7, waiting for transfers between devices, on_device(): held = lax.ppermute(held, 'ex', ring)  31.1 us
    all_to_all x3, starting transfers between devices, over_experts(): return lax.all_to_all(part, 'ex', split_axis=0, concat_axis=0, tiled=True)  29.9 us
    ppermute x1, waiting for transfers between devices, on_device(): sent = lax.ppermute(sent, 'kv', [(i, (i + turn) % kv) for i in range(kv)])  26.8 us
    pallas_call x1, Pallas kernels, attention(): pl.pallas_call(functools.partial(attention_kernel, 1.0 / math.sqrt(HD)),...  23.9 us
  transfers between devices with their start and end apart: 46, of which 24 were waited for; matrix products, arithmetic and copies ran while one was open for 5% of the time, Pallas kernels for 28%

commit v1 on v0

--- a/solution.py
+++ b/solution.py
@@ -319,7 +319,7 @@
         for early in due.get(step, []):
             hiddens[early] = hidden_of(early)
             held, hiddens[early] = lax.optimization_barrier((held, hiddens[early]))
-        if step == min(3, chips - 1):
+        if step == min(4, chips - 1):
             held, downs = lax.optimization_barrier((held, downs))
         blocks[step] = held
     for step in range(chips):

time: 421 us -> 407 us (0.967)
  waiting for transfers between devices: 176 us -> 165 us
    ppermute x3, waiting for transfers between devices: 52.4 us -> 31.9 us  [over_kv(): lax.ppermute(part, 'kv', [(i, (i + turn) % kv) for i in range(kv)])]
    ppermute x7, starting transfers between devices: 20.9 us -> 25.7 us  [on_device(): held = lax.ppermute(held, 'ex', ring)]
    ppermute x14, waiting for transfers between devices: 49.3 us -> 53.8 us  [on_device(): running = lax.ppermute(running, 'ex', ring)]
    ppermute x14, starting transfers between devices: 17.5 us -> 13.2 us  [on_device(): running = lax.ppermute(running, 'ex', ring)]
  transfers between devices with their start and end apart: 46 -> 46, of which waited for: 24 -> 25; matrix products, arithmetic and copies ran while one was open for 5% -> 5% of each run, Pallas kernels for 28% -> 31%
where the time goes in v1:
time: 407 us; the launch traced here: 399 us
  waiting for transfers between devices  165 us (41%)
  Pallas kernels  126 us (31%)
  starting transfers between devices  76.8 us (19%)
  local copies, waits for them, and re-layouts  19.3 us (5%)
  other arithmetic  11.8 us (3%)
    pallas_call x8, Pallas kernels, expert_hidden(): pl.pallas_call(functools.partial(hidden_kernel, experts, width), in_specs...  64.8 us
    ppermute x14, waiting for transfers between devices, on_device(): running = lax.ppermute(running, 'ex', ring)  53.8 us
    ppermute x7, waiting for transfers between devices, on_device(): held = lax.ppermute(held, 'ex', ring)  35 us
    pallas_call x8, Pallas kernels, expert_down(): pl.pallas_call(down_kernel, in_specs=[vmem] * (2 + len(weights)), out_spe...  33.8 us
    ppermute x3, waiting for transfers between devices, over_kv(): lax.ppermute(part, 'kv', [(i, (i + turn) % kv) for i in range(kv)])  31.9 us
    all_to_all x3, starting transfers between devices, over_experts(): return lax.all_to_all(part, 'ex', split_axis=0, concat_axis=0, tiled=True)  29.9 us
    ppermute x1, waiting for transfers between devices, on_device(): sent = lax.ppermute(sent, 'kv', [(i, (i + turn) % kv) for i in range(kv)])  26.8 us
    ppermute x7, starting transfers between devices, on_device(): held = lax.ppermute(held, 'ex', ring)  25.7 us
  transfers between devices with their start and end apart: 46, of which 25 were waited for; matrix products, arithmetic and copies ran while one was open for 5% of the time, Pallas kernels for 31%

profile of v1, /device:TPU:0, one launch (start us, length us, event | category | flops | bytes accessed | tf_op | source)
XLA Modules:
  0.0 399.3 jit_solution(16465661549812288015)
XLA Ops:
  0.0 3.8 fusion
  3.8 7.4 %all-to-all-start = ((bf16[16,128,512]{2,1,0:T(8,128)(2,1)}), bf16[16,128,512]{2,1,0:T(8,128)(2,1)S(1)}, u32[]{:S(2)}, u32[]{:S(2)}) async-start(bf16[16,128,512]{2,1,0:T(8,128)(2,1)} %fusion), calls=%async_computation | async-start | bytes 4194304 | tf_op jit(solution)/shard_map/all_to_all | solution.py:242
  11.2 6.3 %slice_bitcast_fusion = (bf16[16,128,512]{2,1,0:T(8,128)(2,1)}, bf16[16,128,512]{2,1,0:T(8,128)(2,1)}) fusion(f32[16,3,128,512]{3,2,1,0:T(8,128)} %param.17), kind=kLoop, calls=%fused_computation.8 | loop fusion | bytes 8388608 | tf_op jit(solution)/shard_map/convert_element_type | solution.py:261
  19.7 23.9 %attention.1 = f32[576,2048]{1,0:T(8,128)S(1)} custom-call(s32[2]{0:T(128)S(1)} %copy-done.5, bf16[576,2048]{1,0:T(8,128)(2,1)S(1)} %bitcast.22, f32[1,2048]{1,0:T(1,128)S(1)} %bitcast.23, bf16[3,2048,1024]{2,1,0:T(8,128)(2,1)} %bitcast.25, bf16[2,2,512,1024]{3,2,1,0:T(8,128)(2,1)S(1)} %copy-done.2, bf16[1024,2048]{1,0:T(8,128)(2,1)S(1)} %copy-done.3), custom_call_target="tpu_custom_call" | custom-call | flops 10737418240 | bytes 23855104 | tf_op jit(solution)/shard_map/attention/pallas_call | solution.py:76
  45.8 6.5 %all-to-all-done.refs_2_ = bf16[16,128,512]{2,1,0:T(8,128)(2,1)S(1)} async-done(((bf16[16,128,512]{2,1,0:T(8,128)(2,1)}), bf16[16,128,512]{2,1,0:T(8,128)(2,1)S(1)}, u32[]{:S(2)}, u32[]{:S(2)}) %all-to-all-start) | async-done | bytes 2097184 | tf_op jit(solution)/shard_map/all_to_all | solution.py:242
  52.3 11.3 %all-to-all-start.1 = ((bf16[16,128,512]{2,1,0:T(8,128)(2,1)}), bf16[16,128,512]{2,1,0:T(8,128)(2,1)}, u32[]{:S(2)}, u32[]{:S(2)}) async-start(bf16[16,128,512]{2,1,0:T(8,128)(2,1)} %get-tuple-element.78), calls=%async_computation.1 | async-start | bytes 4194304 | tf_op jit(solution)/shard_map/all_to_all | solution.py:242
  67.5 26.8 %collective-permute-done = bf16[288,2048]{1,0:T(8,128)(2,1)} collective-permute-done((bf16[288,2048]{1,0:T(8,128)(2,1)S(1)}, bf16[288,2048]{1,0:T(8,128)(2,1)}, u32[]{:S(2)}, u32[]{:S(2)}) %collective-permute-start) | collective-permute-done | bytes 1179680 | tf_op jit(solution)/shard_map/ppermute | solution.py:276
  94.4 4.3 %bitcast_add_fusion = f32[288,2048]{1,0:T(8,128)} fusion(bf16[288,2048]{1,0:T(8,128)(2,1)} %collective-permute-done, f32[2,288,2048]{2,1,0:T(8,128)} %bitcast.21, s32[]{:T(128)S(6)} %select_n.29, bf16[1,576,2048]{2,1,0:T(8,128)(2,1)} %param.10, s32[]{:T(128)S(6)} %select_n.28), kind=kLoop, calls=%fused_computation.2 | loop fusion | flops 2359296 | bytes 7077896 | tf_op jit(solution)/shard_map/add | solution.py:277
  98.7 6.0 %all-to-all-done.1.refs_3_ = bf16[16,128,512]{2,1,0:T(8,128)(2,1)} async-done(((bf16[16,128,512]{2,1,0:T(8,128)(2,1)}), bf16[16,128,512]{2,1,0:T(8,128)(2,1)}, u32[]{:S(2)}, u32[]{:S(2)}) %all-to-all-start.1) | async-done | bytes 2097184 | tf_op jit(solution)/shard_map/all_to_all | solution.py:242
  104.7 11.3 %all-to-all-start.2 = ((bf16[16,128,512]{2,1,0:T(8,128)(2,1)}), bf16[16,128,512]{2,1,0:T(8,128)(2,1)}, u32[]{:S(2)}, u32[]{:S(2)}) async-start(bf16[16,128,512]{2,1,0:T(8,128)(2,1)} %get-tuple-element.83), calls=%async_computation.2 | async-start | bytes 4194304 | tf_op jit(solution)/shard_map/all_to_all | solution.py:242
  120.7 2.2 concatenate.15
  122.9 15.8 %collective-permute-done.1.refs_4_ = bf16[16,128,512]{2,1,0:T(8,128)(2,1)} collective-permute-done((bf16[16,128,512]{2,1,0:T(8,128)(2,1)S(1)}, bf16[16,128,512]{2,1,0:T(8,128)(2,1)}, u32[]{:S(2)}, u32[]{:S(2)}) %collective-permute-start.1) | collective-permute-done | bytes 2097184 | tf_op jit(solution)/shard_map/ppermute | solution.py:246
  144.3 20.0 %collective-permute-done.3.refs_0_ = bf16[288,2176]{1,0:T(8,128)(2,1)} collective-permute-done((bf16[288,2176]{1,0:T(8,128)(2,1)S(1)}, bf16[288,2176]{1,0:T(8,128)(2,1)}, u32[]{:S(2)}, u32[]{:S(2)}) %collective-permute-start.3) | collective-permute-done | bytes 1253408 | tf_op jit(solution)/shard_map/ppermute | solution.py:310
  164.3 12.9 %collective-permute-start.4 = (bf16[288,2176]{1,0:T(8,128)(2,1)}, bf16[288,2176]{1,0:T(8,128)(2,1)S(1)}, u32[]{:S(2)}, u32[]{:S(2)}) collective-permute-start(bf16[288,2176]{1,0:T(8,128)(2,1)} %collective-permute-done.3.refs_0_), channel_id=1, source_target_pairs={{0,4},{1,3},{4,8},{5,1},{8,12},{9,5},{12,14},{13,9},{14,10},{15,13... | collective-permute-start | bytes 3760136 | tf_op jit(solution)/shard_map/ppermute | solution.py:310
  177.7 12.8 %collective-permute-done.5.refs_5_ = bf16[16,128,512]{2,1,0:T(8,128)(2,1)} collective-permute-done((bf16[16,128,512]{2,1,0:T(8,128)(2,1)}, bf16[16,128,512]{2,1,0:T(8,128)(2,1)}, u32[]{:S(2)}, u32[]{:S(2)}) %collective-permute-start.5) | collective-permute-done | bytes 2097184 | tf_op jit(solution)/shard_map/ppermute | solution.py:246
  192.1 2.8 collective-permute-start.6
  196.4 8.4 %expert_hidden.9 = (bf16[288,1024]{1,0:T(8,128)(2,1)S(1)}, bf16[288,1024]{1,0:T(8,128)(2,1)S(1)}) custom-call(s32[1]{0:T(128)} %bitcast.11.me_ref, bf16[288,2176]{1,0:T(8,128)(2,1)} %collective-permute-done.3.refs_0_, bf16[288,2176]{1,0:T(8,128)(2,1)S(1)} %collective-permute-done.8.refs_1_, bf16[16,128,512]{2,1,0:T(8,128)(2,1)S(1)} %all-to-all-done.refs_2_, ...), custom_call_target="tpu_custom_call" | custom-call | flops 4831838208 | bytes 11927552 | tf_op jit(solution)/shard_map/expert_hidden/pallas_call | solution.py:133
  204.8 8.0 %expert_hidden.8 = (bf16[288,1024]{1,0:T(8,128)(2,1)S(1)}, bf16[288,1024]{1,0:T(8,128)(2,1)S(1)}) custom-call(s32[1]{0:T(128)} %bitcast.11.me_ref, bf16[288,2176]{1,0:T(8,128)(2,1)S(1)} %pad_maximum_fusion.refs_0_, bf16[288,2176]{1,0:T(8,128)(2,1)S(1)} %collective-permute-done.7.refs_1_, bf16[16,128,512]{2,1,0:T(8,128)(2,1)S(1)} %all-to-all-done.refs_2_, ...), custom_call_target="tpu_custom_call" | custom-call | flops 4831838208 | bytes 11927552 | tf_op jit(solution)/shard_map/expert_hidden/pallas_call | solution.py:133
  212.9 2.7 collective-permute-start.9
  215.6 8.1 %expert_hidden.10 = (bf16[288,1024]{1,0:T(8,128)(2,1)S(1)}, bf16[288,1024]{1,0:T(8,128)(2,1)S(1)}) custom-call(s32[1]{0:T(128)} %bitcast.11.me_ref, bf16[288,2176]{1,0:T(8,128)(2,1)S(1)} %collective-permute-done.4.refs_0_, bf16[288,2176]{1,0:T(8,128)(2,1)S(1)} %collective-permute-done.10.refs_1_, bf16[16,128,512]{2,1,0:T(8,128)(2,1)S(1)} %all-to-all-done.refs_2_, ...), custom_call_target="tpu_custom_call" | custom-call | flops 4831838208 | bytes 11927552 | tf_op jit(solution)/shard_map/expert_hidden/pallas_call | solution.py:133
  223.6 6.5 %collective-permute-done.9.refs_0_ = bf16[288,2176]{1,0:T(8,128)(2,1)S(1)} collective-permute-done((bf16[288,2176]{1,0:T(8,128)(2,1)S(1)}, bf16[288,2176]{1,0:T(8,128)(2,1)S(1)}, u32[]{:S(2)}, u32[]{:S(2)}) %collective-permute-start.9) | collective-permute-done | bytes 1253408 | tf_op jit(solution)/shard_map/ppermute | solution.py:310
  230.2 8.1 %expert_hidden.11 = (bf16[288,1024]{1,0:T(8,128)(2,1)S(1)}, bf16[288,1024]{1,0:T(8,128)(2,1)S(1)}) custom-call(s32[1]{0:T(128)} %bitcast.11.me_ref, bf16[288,2176]{1,0:T(8,128)(2,1)S(1)} %collective-permute-done.6.refs_0_, bf16[288,2176]{1,0:T(8,128)(2,1)S(1)} %collective-permute-done.11.refs_1_, bf16[16,128,512]{2,1,0:T(8,128)(2,1)S(1)} %all-to-all-done.refs_2_, ...), custom_call_target="tpu_custom_call" | custom-call | flops 4831838208 | bytes 11927552 | tf_op jit(solution)/shard_map/expert_hidden/pallas_call | solution.py:133
  238.2 3.3 collective-permute-done.12.refs_3_
  241.6 2.2 collective-permute-start.14
  244.5 8.1 %expert_hidden.12 = (bf16[288,1024]{1,0:T(8,128)(2,1)S(1)}, bf16[288,1024]{1,0:T(8,128)(2,1)S(1)}) custom-call(s32[1]{0:T(128)} %bitcast.11.me_ref, bf16[288,2176]{1,0:T(8,128)(2,1)S(1)} %collective-permute-done.9.refs_0_, bf16[288,2176]{1,0:T(8,128)(2,1)S(1)} %collective-permute-done.15.refs_1_, bf16[16,128,512]{2,1,0:T(8,128)(2,1)S(1)} %all-to-all-done.refs_2_, ...), custom_call_target="tpu_custom_call" | custom-call | flops 4831838208 | bytes 11927552 | tf_op jit(solution)/shard_map/expert_hidden/pallas_call | solution.py:133
  252.6 6.4 %collective-permute-done.14.refs_0_ = bf16[288,2176]{1,0:T(8,128)(2,1)S(1)} collective-permute-done((bf16[288,2176]{1,0:T(8,128)(2,1)S(1)}, bf16[288,2176]{1,0:T(8,128)(2,1)S(1)}, u32[]{:S(2)}, u32[]{:S(2)}) %collective-permute-start.14) | collective-permute-done | bytes 1253408 | tf_op jit(solution)/shard_map/ppermute | solution.py:310
  259.0 4.2 %expert_down.15 = (bf16[288,2048]{1,0:T(8,128)(2,1)S(1)}, bf16[288,2048]{1,0:T(8,128)(2,1)S(1)}) custom-call(bf16[288,1024]{1,0:T(8,128)(2,1)S(1)} %get-tuple-element.141.refs_0_, bf16[288,1024]{1,0:T(8,128)(2,1)S(1)} %get-tuple-element.142.refs_1_, bf16[16,128,512]{2,1,0:T(8,128)(2,1)} %all-to-all-done.2.refs_2_, ...), custom_call_target="tpu_custom_call" | custom-call | flops 2415919104 | bytes 7733248 | tf_op jit(solution)/shard_map/expert_down/pallas_call | solution.py:172
  265.6 4.2 %expert_down.14 = (bf16[288,2048]{1,0:T(8,128)(2,1)S(1)}, bf16[288,2048]{1,0:T(8,128)(2,1)S(1)}) custom-call(bf16[288,1024]{1,0:T(8,128)(2,1)S(1)} %get-tuple-element.137.refs_0_, bf16[288,1024]{1,0:T(8,128)(2,1)S(1)} %get-tuple-element.138.refs_1_, bf16[16,128,512]{2,1,0:T(8,128)(2,1)} %all-to-all-done.2.refs_2_, ...), custom_call_target="tpu_custom_call" | custom-call | flops 2415919104 | bytes 7733248 | tf_op jit(solution)/shard_map/expert_down/pallas_call | solution.py:172
  269.9 4.2 %expert_down.13 = (bf16[288,2048]{1,0:T(8,128)(2,1)S(1)}, bf16[288,2048]{1,0:T(8,128)(2,1)S(1)}) custom-call(bf16[288,1024]{1,0:T(8,128)(2,1)S(1)} %get-tuple-element.133.refs_0_, bf16[288,1024]{1,0:T(8,128)(2,1)S(1)} %get-tuple-element.134.refs_1_, bf16[16,128,512]{2,1,0:T(8,128)(2,1)} %all-to-all-done.2.refs_2_, ...), custom_call_target="tpu_custom_call" | custom-call | flops 2415919104 | bytes 7733248 | tf_op jit(solution)/shard_map/expert_down/pallas_call | solution.py:172
  276.7 8.0 %expert_hidden.13 = (bf16[288,1024]{1,0:T(8,128)(2,1)S(1)}, bf16[288,1024]{1,0:T(8,128)(2,1)S(1)}) custom-call(s32[1]{0:T(128)} %bitcast.11.me_ref, bf16[288,2176]{1,0:T(8,128)(2,1)S(1)} %collective-permute-done.14.refs_0_, bf16[288,2176]{1,0:T(8,128)(2,1)S(1)} %collective-permute-done.17.refs_1_, bf16[16,128,512]{2,1,0:T(8,128)(2,1)S(1)} %all-to-all-done.refs_2_, ...), custom_call_target="tpu_custom_call" | custom-call | flops 4831838208 | bytes 11927552 | tf_op jit(solution)/shard_map/expert_hidden/pallas_call | solution.py:133
  290.8 4.2 %expert_down.12 = (bf16[288,2048]{1,0:T(8,128)(2,1)S(1)}, bf16[288,2048]{1,0:T(8,128)(2,1)S(1)}) custom-call(bf16[288,1024]{1,0:T(8,128)(2,1)S(1)} %get-tuple-element.129.refs_0_, bf16[288,1024]{1,0:T(8,128)(2,1)S(1)} %get-tuple-element.130.refs_1_, bf16[16,128,512]{2,1,0:T(8,128)(2,1)} %all-to-all-done.2.refs_2_, ...), custom_call_target="tpu_custom_call" | custom-call | flops 2415919104 | bytes 7733248 | tf_op jit(solution)/shard_map/expert_down/pallas_call | solution.py:172
  295.5 5.8 %collective-permute-done.29.refs_2_ = bf16[288,1024]{1,0:T(8,128)(2,1)S(1)} collective-permute-done((bf16[288,1024]{1,0:T(8,128)(2,1)S(1)}, bf16[288,1024]{1,0:T(8,128)(2,1)S(1)}, u32[]{:S(2)}, u32[]{:S(2)}) %collective-permute-start.29) | collective-permute-done | bytes 589856 | tf_op jit(solution)/shard_map/ppermute | solution.py:342
  301.8 4.2 %expert_down.11 = (bf16[288,2048]{1,0:T(8,128)(2,1)S(1)}, bf16[288,2048]{1,0:T(8,128)(2,1)S(1)}) custom-call(bf16[288,1024]{1,0:T(8,128)(2,1)S(1)} %get-tuple-element.125.refs_0_, bf16[288,1024]{1,0:T(8,128)(2,1)S(1)} %get-tuple-element.126.refs_1_, bf16[16,128,512]{2,1,0:T(8,128)(2,1)} %all-to-all-done.2.refs_2_, ...), custom_call_target="tpu_custom_call" | custom-call | flops 2415919104 | bytes 7733248 | tf_op jit(solution)/shard_map/expert_down/pallas_call | solution.py:172
  306.1 8.1 %expert_hidden.14 = (bf16[288,1024]{1,0:T(8,128)(2,1)S(1)}, bf16[288,1024]{1,0:T(8,128)(2,1)S(1)}) custom-call(s32[1]{0:T(128)} %bitcast.11.me_ref, bf16[288,2176]{1,0:T(8,128)(2,1)S(1)} %collective-permute-done.16.refs_0_, bf16[288,2176]{1,0:T(8,128)(2,1)S(1)} %collective-permute-done.19.refs_1_, bf16[16,128,512]{2,1,0:T(8,128)(2,1)S(1)} %all-to-all-done.refs_2_, ...), custom_call_target="tpu_custom_call" | custom-call | flops 4831838208 | bytes 11927552 | tf_op jit(solution)/shard_map/expert_hidden/pallas_call | solution.py:133
  314.7 6.3 %collective-permute-done.36.refs_2_ = bf16[288,1024]{1,0:T(8,128)(2,1)S(1)} collective-permute-done((bf16[288,1024]{1,0:T(8,128)(2,1)S(1)}, bf16[288,1024]{1,0:T(8,128)(2,1)S(1)}, u32[]{:S(2)}, u32[]{:S(2)}) %collective-permute-start.36) | collective-permute-done | bytes 589856 | tf_op jit(solution)/shard_map/ppermute | solution.py:342
  321.5 5.8 %collective-permute-done.30.refs_2_ = bf16[288,1024]{1,0:T(8,128)(2,1)S(1)} collective-permute-done((bf16[288,1024]{1,0:T(8,128)(2,1)S(1)}, bf16[288,1024]{1,0:T(8,128)(2,1)S(1)}, u32[]{:S(2)}, u32[]{:S(2)}) %collective-permute-start.30) | collective-permute-done | bytes 589856 | tf_op jit(solution)/shard_map/ppermute | solution.py:342
  327.9 5.8 %collective-permute-done.37.refs_2_ = bf16[288,1024]{1,0:T(8,128)(2,1)S(1)} collective-permute-done((bf16[288,1024]{1,0:T(8,128)(2,1)S(1)}, bf16[288,1024]{1,0:T(8,128)(2,1)S(1)}, u32[]{:S(2)}, u32[]{:S(2)}) %collective-permute-start.37) | collective-permute-done | bytes 589856 | tf_op jit(solution)/shard_map/ppermute | solution.py:342
  334.2 5.8 %collective-permute-done.31.refs_2_ = bf16[288,1024]{1,0:T(8,128)(2,1)S(1)} collective-permute-done((bf16[288,1024]{1,0:T(8,128)(2,1)S(1)}, bf16[288,1024]{1,0:T(8,128)(2,1)S(1)}, u32[]{:S(2)}, u32[]{:S(2)}) %collective-permute-start.31) | collective-permute-done | bytes 589856 | tf_op jit(solution)/shard_map/ppermute | solution.py:342
  340.7 4.2 %expert_down.10 = (bf16[288,2048]{1,0:T(8,128)(2,1)S(1)}, bf16[288,2048]{1,0:T(8,128)(2,1)S(1)}) custom-call(bf16[288,1024]{1,0:T(8,128)(2,1)S(1)} %get-tuple-element.121.refs_0_, bf16[288,1024]{1,0:T(8,128)(2,1)S(1)} %get-tuple-element.122.refs_1_, bf16[16,128,512]{2,1,0:T(8,128)(2,1)} %all-to-all-done.2.refs_2_, ...), custom_call_target="tpu_custom_call" | custom-call | flops 2415919104 | bytes 7733248 | tf_op jit(solution)/shard_map/expert_down/pallas_call | solution.py:172
  345.0 8.0 %expert_hidden.15 = (bf16[288,1024]{1,0:T(8,128)(2,1)S(1)}, bf16[288,1024]{1,0:T(8,128)(2,1)S(1)}) custom-call(s32[1]{0:T(128)} %bitcast.11.me_ref, bf16[288,2176]{1,0:T(8,128)(2,1)S(1)} %collective-permute-done.18.refs_0_, bf16[288,2176]{1,0:T(8,128)(2,1)S(1)} %collective-permute-done.20.refs_1_, bf16[16,128,512]{2,1,0:T(8,128)(2,1)S(1)} %all-to-all-done.refs_2_, ...), custom_call_target="tpu_custom_call" | custom-call | flops 4831838208 | bytes 11927552 | tf_op jit(solution)/shard_map/expert_hidden/pallas_call | solution.py:133
  353.1 4.2 %expert_down.9 = (bf16[288,2048]{1,0:T(8,128)(2,1)S(1)}, bf16[288,2048]{1,0:T(8,128)(2,1)S(1)}) custom-call(bf16[288,1024]{1,0:T(8,128)(2,1)S(1)} %get-tuple-element.117.refs_0_, bf16[288,1024]{1,0:T(8,128)(2,1)S(1)} %get-tuple-element.118.refs_1_, bf16[16,128,512]{2,1,0:T(8,128)(2,1)} %all-to-all-done.2.refs_2_, ...), custom_call_target="tpu_custom_call" | custom-call | flops 2415919104 | bytes 7733248 | tf_op jit(solution)/shard_map/expert_down/pallas_call | solution.py:172
  359.8 4.2 %expert_down.8 = (bf16[288,2048]{1,0:T(8,128)(2,1)S(1)}, bf16[288,2048]{1,0:T(8,128)(2,1)S(1)}) custom-call(bf16[288,1024]{1,0:T(8,128)(2,1)S(1)} %get-tuple-element.91.refs_0_, bf16[288,1024]{1,0:T(8,128)(2,1)S(1)} %get-tuple-element.92.refs_1_, bf16[16,128,512]{2,1,0:T(8,128)(2,1)} %all-to-all-done.2.refs_2_, ...), custom_call_target="tpu_custom_call" | custom-call | flops 2415919104 | bytes 7733248 | tf_op jit(solution)/shard_map/expert_down/pallas_call | solution.py:172
  364.8 3.2 collective-permute-done.39.refs_2_
  370.0 4.4 %collective-permute-done.33.refs_2_ = bf16[288,1024]{1,0:T(8,128)(2,1)S(1)} collective-permute-done((bf16[288,1024]{1,0:T(8,128)(2,1)S(1)}, bf16[288,1024]{1,0:T(8,128)(2,1)S(1)}, u32[]{:S(2)}, u32[]{:S(2)}) %collective-permute-start.33) | collective-permute-done | bytes 589856 | tf_op jit(solution)/shard_map/ppermute | solution.py:342
  376.3 4.4 %collective-permute-done.40.refs_2_ = bf16[288,1024]{1,0:T(8,128)(2,1)S(1)} collective-permute-done((bf16[288,1024]{1,0:T(8,128)(2,1)S(1)}, bf16[288,1024]{1,0:T(8,128)(2,1)S(1)}, u32[]{:S(2)}, u32[]{:S(2)}) %collective-permute-start.40) | collective-permute-done | bytes 589856 | tf_op jit(solution)/shard_map/ppermute | solution.py:342
  382.6 4.4 %collective-permute-done.34.refs_2_ = bf16[288,1024]{1,0:T(8,128)(2,1)S(1)} collective-permute-done((bf16[288,1024]{1,0:T(8,128)(2,1)S(1)}, bf16[288,1024]{1,0:T(8,128)(2,1)S(1)}, u32[]{:S(2)}, u32[]{:S(2)}) %collective-permute-start.34) | collective-permute-done | bytes 589856 | tf_op jit(solution)/shard_map/ppermute | solution.py:342
  387.2 6.1 %collective-permute-done.41.refs_2_ = bf16[288,1024]{1,0:T(8,128)(2,1)S(1)} collective-permute-done((bf16[288,1024]{1,0:T(8,128)(2,1)S(1)}, bf16[288,1024]{1,0:T(8,128)(2,1)S(1)}, u32[]{:S(2)}, u32[]{:S(2)}) %collective-permute-start.41) | collective-permute-done | bytes 589856 | tf_op jit(solution)/shard_map/ppermute | solution.py:342
  395.7 3.2 fusion.2
  (118 shorter events, 49.6 us)
Async XLA Ops:
  3.8 48.5 %all-to-all-start = ((bf16[16,128,512]{2,1,0:T(8,128)(2,1)}), bf16[16,128,512]{2,1,0:T(8,128)(2,1)S(1)}, u32[]{:S(2)}, u32[]{:S(2)}) async-start(bf16[16,128,512]{2,1,0:T(8,128)(2,1)} %fusion), calls=%async_computation | async-start | bytes 4194304 | tf_op jit(solution)/shard_map/all_to_all | solution.py:242
  11.2 6.4 %copy-start.1 = (bf16[1,576,2048]{2,1,0:T(8,128)(2,1)S(1)}, bf16[1,576,2048]{2,1,0:T(8,128)(2,1)}, u32[]{:S(2)}) copy-start(bf16[1,576,2048]{2,1,0:T(8,128)(2,1)} %param.10) | copy-start | bytes 7077892
  52.3 52.4 %all-to-all-start.1 = ((bf16[16,128,512]{2,1,0:T(8,128)(2,1)}), bf16[16,128,512]{2,1,0:T(8,128)(2,1)}, u32[]{:S(2)}, u32[]{:S(2)}) async-start(bf16[16,128,512]{2,1,0:T(8,128)(2,1)} %get-tuple-element.78), calls=%async_computation.1 | async-start | bytes 4194304 | tf_op jit(solution)/shard_map/all_to_all | solution.py:242
  65.4 29.0 %collective-permute-start = (bf16[288,2048]{1,0:T(8,128)(2,1)S(1)}, bf16[288,2048]{1,0:T(8,128)(2,1)}, u32[]{:S(2)}, u32[]{:S(2)}) collective-permute-start(bf16[288,2048]{1,0:T(8,128)(2,1)S(1)} %fusion.1), channel_id=1, source_target_pairs={{0,16},{16,0},{1,17},{17,1},{2,18},{18,2},{3,19},{19,3},{4,20},{20... | collective-permute-start | bytes 3538952 | tf_op jit(solution)/shard_map/ppermute | solution.py:276
  67.0 71.8 %collective-permute-start.1 = (bf16[16,128,512]{2,1,0:T(8,128)(2,1)S(1)}, bf16[16,128,512]{2,1,0:T(8,128)(2,1)}, u32[]{:S(2)}, u32[]{:S(2)}) collective-permute-start(bf16[16,128,512]{2,1,0:T(8,128)(2,1)S(1)} %all-to-all-done.refs_2_), channel_id=1, source_target_pairs={{0,16},{16,0},{1,17},{17,1},{2,18},{18,2},{3,19},{19,3},{4,20},{20... | collective-permute-start | bytes 6291464 | tf_op jit(solution)/shard_map/ppermute | solution.py:246
  98.7 17.3 %copy-start.8 = (s32[1,288,8]{1,2,0:T(8,128)S(1)}, s32[1,288,8]{1,2,0:T(8,128)}, u32[]{:S(2)}) copy-start(s32[1,288,8]{1,2,0:T(8,128)} %param.18) | copy-start | bytes 27652
  104.7 59.6 %all-to-all-start.2 = ((bf16[16,128,512]{2,1,0:T(8,128)(2,1)}), bf16[16,128,512]{2,1,0:T(8,128)(2,1)}, u32[]{:S(2)}, u32[]{:S(2)}) async-start(bf16[16,128,512]{2,1,0:T(8,128)(2,1)} %get-tuple-element.83), calls=%async_computation.2 | async-start | bytes 4194304 | tf_op jit(solution)/shard_map/all_to_all | solution.py:242
  138.9 2.1 collective-permute-start.2
  141.1 23.2 %collective-permute-start.3 = (bf16[288,2176]{1,0:T(8,128)(2,1)S(1)}, bf16[288,2176]{1,0:T(8,128)(2,1)}, u32[]{:S(2)}, u32[]{:S(2)}) collective-permute-start(bf16[288,2176]{1,0:T(8,128)(2,1)S(1)} %pad_maximum_fusion.refs_0_), channel_id=1, source_target_pairs={{0,4},{1,3},{4,8},{5,1},{8,12},{9,5},{12,14},{13,9},{14,10},{15,13... | collective-permute-start | bytes 3760136 | tf_op jit(solution)/shard_map/ppermute | solution.py:310
  142.8 47.7 %collective-permute-start.5 = (bf16[16,128,512]{2,1,0:T(8,128)(2,1)}, bf16[16,128,512]{2,1,0:T(8,128)(2,1)}, u32[]{:S(2)}, u32[]{:S(2)}) collective-permute-start(bf16[16,128,512]{2,1,0:T(8,128)(2,1)} %all-to-all-done.1.refs_3_), channel_id=1, source_target_pairs={{0,16},{16,0},{1,17},{17,1},{2,18},{18,2},{3,19},{19,3},{4,20},{20... | collective-permute-start | bytes 6291464 | tf_op jit(solution)/shard_map/ppermute | solution.py:246
  164.3 27.8 %collective-permute-start.4 = (bf16[288,2176]{1,0:T(8,128)(2,1)}, bf16[288,2176]{1,0:T(8,128)(2,1)S(1)}, u32[]{:S(2)}, u32[]{:S(2)}) collective-permute-start(bf16[288,2176]{1,0:T(8,128)(2,1)} %collective-permute-done.3.refs_0_), channel_id=1, source_target_pairs={{0,4},{1,3},{4,8},{5,1},{8,12},{9,5},{12,14},{13,9},{14,10},{15,13... | collective-permute-start | bytes 3760136 | tf_op jit(solution)/shard_map/ppermute | solution.py:310
  177.2 19.1 %collective-permute-start.8 = (bf16[288,2176]{1,0:T(8,128)(2,1)}, bf16[288,2176]{1,0:T(8,128)(2,1)S(1)}, u32[]{:S(2)}, u32[]{:S(2)}) collective-permute-start(bf16[288,2176]{1,0:T(8,128)(2,1)} %collective-permute-done.3.refs_0_), channel_id=1, source_target_pairs={{0,1},{1,0},{2,3},{3,2},{4,5},{5,4},{6,7},{7,6},{8,9},{9,8},{10,11... | collective-permute-start | bytes 3760136 | tf_op jit(solution)/shard_map/ppermute | solution.py:306
  177.2 27.6 %collective-permute-start.7 = (bf16[288,2176]{1,0:T(8,128)(2,1)S(1)}, bf16[288,2176]{1,0:T(8,128)(2,1)S(1)}, u32[]{:S(2)}, u32[]{:S(2)}) collective-permute-start(bf16[288,2176]{1,0:T(8,128)(2,1)S(1)} %pad_maximum_fusion.refs_0_), channel_id=1, source_target_pairs={{0,1},{1,0},{2,3},{3,2},{4,5},{5,4},{6,7},{7,6},{8,9},{9,8},{10,11... | collective-permute-start | bytes 3760136 | tf_op jit(solution)/shard_map/ppermute | solution.py:306
  192.1 20.8 %collective-permute-start.6 = (bf16[288,2176]{1,0:T(8,128)(2,1)S(1)}, bf16[288,2176]{1,0:T(8,128)(2,1)S(1)}, u32[]{:S(2)}, u32[]{:S(2)}) collective-permute-start(bf16[288,2176]{1,0:T(8,128)(2,1)S(1)} %collective-permute-done.4.refs_0_), channel_id=1, source_target_pairs={{0,4},{1,3},{4,8},{5,1},{8,12},{9,5},{12,14},{13,9},{14,10},{15,13... | collective-permute-start | bytes 3760136 | tf_op jit(solution)/shard_map/ppermute | solution.py:310
  194.8 46.7 %collective-permute-start.12 = (bf16[16,128,512]{2,1,0:T(8,128)(2,1)}, bf16[16,128,512]{2,1,0:T(8,128)(2,1)S(1)}, u32[]{:S(2)}, u32[]{:S(2)}) collective-permute-start(bf16[16,128,512]{2,1,0:T(8,128)(2,1)} %all-to-all-done.2.refs_2_), channel_id=1, source_target_pairs={{0,16},{16,0},{1,17},{17,1},{2,18},{18,2},{3,19},{19,3},{4,20},{20... | collective-permute-start | bytes 6291464 | tf_op jit(solution)/shard_map/ppermute | solution.py:246
  196.4 19.2 %collective-permute-start.10 = (bf16[288,2176]{1,0:T(8,128)(2,1)S(1)}, bf16[288,2176]{1,0:T(8,128)(2,1)S(1)}, u32[]{:S(2)}, u32[]{:S(2)}) collective-permute-start(bf16[288,2176]{1,0:T(8,128)(2,1)S(1)} %collective-permute-done.4.refs_0_), channel_id=1, source_target_pairs={{0,1},{1,0},{2,3},{3,2},{4,5},{5,4},{6,7},{7,6},{8,9},{9,8},{10,11... | collective-permute-start | bytes 3760136 | tf_op jit(solution)/shard_map/ppermute | solution.py:306
  212.9 17.3 %collective-permute-start.9 = (bf16[288,2176]{1,0:T(8,128)(2,1)S(1)}, bf16[288,2176]{1,0:T(8,128)(2,1)S(1)}, u32[]{:S(2)}, u32[]{:S(2)}) collective-permute-start(bf16[288,2176]{1,0:T(8,128)(2,1)S(1)} %collective-permute-done.6.refs_0_), channel_id=1, source_target_pairs={{0,4},{1,3},{4,8},{5,1},{8,12},{9,5},{12,14},{13,9},{14,10},{15,13... | collective-permute-start | bytes 3760136 | tf_op jit(solution)/shard_map/ppermute | solution.py:310
  215.6 14.6 %collective-permute-start.11 = (bf16[288,2176]{1,0:T(8,128)(2,1)S(1)}, bf16[288,2176]{1,0:T(8,128)(2,1)S(1)}, u32[]{:S(2)}, u32[]{:S(2)}) collective-permute-start(bf16[288,2176]{1,0:T(8,128)(2,1)S(1)} %collective-permute-done.6.refs_0_), channel_id=1, source_target_pairs={{0,1},{1,0},{2,3},{3,2},{4,5},{5,4},{6,7},{7,6},{8,9},{9,8},{10,11... | collective-permute-start | bytes 3760136 | tf_op jit(solution)/shard_map/ppermute | solution.py:306
  241.6 3.0 collective-permute-start.15
  241.6 17.4 %collective-permute-start.14 = (bf16[288,2176]{1,0:T(8,128)(2,1)S(1)}, bf16[288,2176]{1,0:T(8,128)(2,1)S(1)}, u32[]{:S(2)}, u32[]{:S(2)}) collective-permute-start(bf16[288,2176]{1,0:T(8,128)(2,1)S(1)} %collective-permute-done.9.refs_0_), channel_id=1, source_target_pairs={{0,4},{1,3},{4,8},{5,1},{8,12},{9,5},{12,14},{13,9},{14,10},{15,13... | collective-permute-start | bytes 3760136 | tf_op jit(solution)/shard_map/ppermute | solution.py:310
  259.0 17.7 %collective-permute-start.17 = (bf16[288,2176]{1,0:T(8,128)(2,1)S(1)}, bf16[288,2176]{1,0:T(8,128)(2,1)S(1)}, u32[]{:S(2)}, u32[]{:S(2)}) collective-permute-start(bf16[288,2176]{1,0:T(8,128)(2,1)S(1)} %collective-permute-done.14.refs_0_), channel_id=1, source_target_pairs={{0,1},{1,0},{2,3},{3,2},{4,5},{5,4},{6,7},{7,6},{8,9},{9,8},{10,11... | collective-permute-start | bytes 3760136 | tf_op jit(solution)/shard_map/ppermute | solution.py:306
  263.2 11.4 %collective-permute-start.27 = (bf16[288,2048]{1,0:T(8,128)(2,1)S(1)}, bf16[288,2048]{1,0:T(8,128)(2,1)S(1)}, u32[]{:S(2)}, u32[]{:S(2)}) collective-permute-start(bf16[288,2048]{1,0:T(8,128)(2,1)S(1)} %get-tuple-element.144), channel_id=1, source_target_pairs={{0,1},{1,0},{2,3},{3,2},{4,5},{5,4},{6,7},{7,6},{8,9},{9,8},{10,11... | collective-permute-start | bytes 3538952 | tf_op jit(solution)/shard_map/ppermute | solution.py:333
  263.8 20.9 %collective-permute-start.16 = (bf16[288,2176]{1,0:T(8,128)(2,1)S(1)}, bf16[288,2176]{1,0:T(8,128)(2,1)S(1)}, u32[]{:S(2)}, u32[]{:S(2)}) collective-permute-start(bf16[288,2176]{1,0:T(8,128)(2,1)S(1)} %collective-permute-done.14.refs_0_), channel_id=1, source_target_pairs={{0,4},{1,3},{4,8},{5,1},{8,12},{9,5},{12,14},{13,9},{14,10},{15,13... | collective-permute-start | bytes 3760136 | tf_op jit(solution)/shard_map/ppermute | solution.py:310
  269.8 15.3 %collective-permute-start.26 = (bf16[288,2048]{1,0:T(8,128)(2,1)S(1)}, bf16[288,2048]{1,0:T(8,128)(2,1)S(1)}, u32[]{:S(2)}, u32[]{:S(2)}) collective-permute-start(bf16[288,2048]{1,0:T(8,128)(2,1)S(1)} %get-tuple-element.140), channel_id=1, source_target_pairs={{0,1},{1,0},{2,3},{3,2},{4,5},{5,4},{6,7},{7,6},{8,9},{9,8},{10,11... | collective-permute-start | bytes 3538952 | tf_op jit(solution)/shard_map/ppermute | solution.py:333
  274.1 21.3 %collective-permute-start.25 = (bf16[288,2048]{1,0:T(8,128)(2,1)S(1)}, bf16[288,2048]{1,0:T(8,128)(2,1)S(1)}, u32[]{:S(2)}, u32[]{:S(2)}) collective-permute-start(bf16[288,2048]{1,0:T(8,128)(2,1)S(1)} %get-tuple-element.136), channel_id=1, source_target_pairs={{0,1},{1,0},{2,3},{3,2},{4,5},{5,4},{6,7},{7,6},{8,9},{9,8},{10,11... | collective-permute-start | bytes 3538952 | tf_op jit(solution)/shard_map/ppermute | solution.py:333
  274.8 12.3 %collective-permute-start.28 = (bf16[288,1024]{1,0:T(8,128)(2,1)S(1)}, bf16[288,1024]{1,0:T(8,128)(2,1)S(1)}, u32[]{:S(2)}, u32[]{:S(2)}) collective-permute-start(bf16[288,1024]{1,0:T(8,128)(2,1)S(1)} %add_terms.16), channel_id=1, source_target_pairs={{0,4},{1,3},{4,8},{5,1},{8,12},{9,5},{12,14},{13,9},{14,10},{15,13... | collective-permute-start | bytes 1769480 | tf_op jit(solution)/shard_map/ppermute | solution.py:342
  284.8 21.3 %collective-permute-start.19 = (bf16[288,2176]{1,0:T(8,128)(2,1)S(1)}, bf16[288,2176]{1,0:T(8,128)(2,1)S(1)}, u32[]{:S(2)}, u32[]{:S(2)}) collective-permute-start(bf16[288,2176]{1,0:T(8,128)(2,1)S(1)} %collective-permute-done.16.refs_0_), channel_id=1, source_target_pairs={{0,1},{1,0},{2,3},{3,2},{4,5},{5,4},{6,7},{7,6},{8,9},{9,8},{10,11... | collective-permute-start | bytes 3760136 | tf_op jit(solution)/shard_map/ppermute | solution.py:306
  285.0 10.1 %collective-permute-start.35 = (bf16[288,1024]{1,0:T(8,128)(2,1)S(1)}, bf16[288,1024]{1,0:T(8,128)(2,1)S(1)}, u32[]{:S(2)}, u32[]{:S(2)}) collective-permute-start(bf16[288,1024]{1,0:T(8,128)(2,1)S(1)} %add_terms.24), channel_id=1, source_target_pairs={{0,4},{1,3},{4,8},{5,1},{8,12},{9,5},{12,14},{13,9},{14,10},{15,13... | collective-permute-start | bytes 1769480 | tf_op jit(solution)/shard_map/ppermute | solution.py:342
  287.3 13.9 %collective-permute-start.29 = (bf16[288,1024]{1,0:T(8,128)(2,1)S(1)}, bf16[288,1024]{1,0:T(8,128)(2,1)S(1)}, u32[]{:S(2)}, u32[]{:S(2)}) collective-permute-start(bf16[288,1024]{1,0:T(8,128)(2,1)S(1)} %add_terms.17), channel_id=1, source_target_pairs={{0,4},{1,3},{4,8},{5,1},{8,12},{9,5},{12,14},{13,9},{14,10},{15,13... | collective-permute-start | bytes 1769480 | tf_op jit(solution)/shard_map/ppermute | solution.py:342
  289.1 25.5 %collective-permute-start.18 = (bf16[288,2176]{1,0:T(8,128)(2,1)S(1)}, bf16[288,2176]{1,0:T(8,128)(2,1)S(1)}, u32[]{:S(2)}, u32[]{:S(2)}) collective-permute-start(bf16[288,2176]{1,0:T(8,128)(2,1)S(1)} %collective-permute-done.16.refs_0_), channel_id=1, source_target_pairs={{0,4},{1,3},{4,8},{5,1},{8,12},{9,5},{12,14},{13,9},{14,10},{15,13... | collective-permute-start | bytes 3760136 | tf_op jit(solution)/shard_map/ppermute | solution.py:310
  295.1 26.5 %collective-permute-start.24 = (bf16[288,2048]{1,0:T(8,128)(2,1)S(1)}, bf16[288,2048]{1,0:T(8,128)(2,1)S(1)}, u32[]{:S(2)}, u32[]{:S(2)}) collective-permute-start(bf16[288,2048]{1,0:T(8,128)(2,1)S(1)} %get-tuple-element.132), channel_id=1, source_target_pairs={{0,1},{1,0},{2,3},{3,2},{4,5},{5,4},{6,7},{7,6},{8,9},{9,8},{10,11... | collective-permute-start | bytes 3538952 | tf_op jit(solution)/shard_map/ppermute | solution.py:333
  295.4 25.6 %collective-permute-start.36 = (bf16[288,1024]{1,0:T(8,128)(2,1)S(1)}, bf16[288,1024]{1,0:T(8,128)(2,1)S(1)}, u32[]{:S(2)}, u32[]{:S(2)}) collective-permute-start(bf16[288,1024]{1,0:T(8,128)(2,1)S(1)} %add_terms.25), channel_id=1, source_target_pairs={{0,4},{1,3},{4,8},{5,1},{8,12},{9,5},{12,14},{13,9},{14,10},{15,13... | collective-permute-start | bytes 1769480 | tf_op jit(solution)/shard_map/ppermute | solution.py:342
  301.5 25.9 %collective-permute-start.30 = (bf16[288,1024]{1,0:T(8,128)(2,1)S(1)}, bf16[288,1024]{1,0:T(8,128)(2,1)S(1)}, u32[]{:S(2)}, u32[]{:S(2)}) collective-permute-start(bf16[288,1024]{1,0:T(8,128)(2,1)S(1)} %add_terms.18), channel_id=1, source_target_pairs={{0,4},{1,3},{4,8},{5,1},{8,12},{9,5},{12,14},{13,9},{14,10},{15,13... | collective-permute-start | bytes 1769480 | tf_op jit(solution)/shard_map/ppermute | solution.py:342
  306.0 33.9 %collective-permute-start.23 = (bf16[288,2048]{1,0:T(8,128)(2,1)S(1)}, bf16[288,2048]{1,0:T(8,128)(2,1)S(1)}, u32[]{:S(2)}, u32[]{:S(2)}) collective-permute-start(bf16[288,2048]{1,0:T(8,128)(2,1)S(1)} %get-tuple-element.128), channel_id=1, source_target_pairs={{0,1},{1,0},{2,3},{3,2},{4,5},{5,4},{6,7},{7,6},{8,9},{9,8},{10,11... | collective-permute-start | bytes 3538952 | tf_op jit(solution)/shard_map/ppermute | solution.py:333
  314.7 30.3 %collective-permute-start.20 = (bf16[288,2176]{1,0:T(8,128)(2,1)S(1)}, bf16[288,2176]{1,0:T(8,128)(2,1)S(1)}, u32[]{:S(2)}, u32[]{:S(2)}) collective-permute-start(bf16[288,2176]{1,0:T(8,128)(2,1)S(1)} %collective-permute-done.18.refs_0_), channel_id=1, source_target_pairs={{0,1},{1,0},{2,3},{3,2},{4,5},{5,4},{6,7},{7,6},{8,9},{9,8},{10,11... | collective-permute-start | bytes 3760136 | tf_op jit(solution)/shard_map/ppermute | solution.py:306
  321.2 12.4 %collective-permute-start.37 = (bf16[288,1024]{1,0:T(8,128)(2,1)S(1)}, bf16[288,1024]{1,0:T(8,128)(2,1)S(1)}, u32[]{:S(2)}, u32[]{:S(2)}) collective-permute-start(bf16[288,1024]{1,0:T(8,128)(2,1)S(1)} %add_terms.26), channel_id=1, source_target_pairs={{0,4},{1,3},{4,8},{5,1},{8,12},{9,5},{12,14},{13,9},{14,10},{15,13... | collective-permute-start | bytes 1769480 | tf_op jit(solution)/shard_map/ppermute | solution.py:342
  327.5 12.4 %collective-permute-start.31 = (bf16[288,1024]{1,0:T(8,128)(2,1)S(1)}, bf16[288,1024]{1,0:T(8,128)(2,1)S(1)}, u32[]{:S(2)}, u32[]{:S(2)}) collective-permute-start(bf16[288,1024]{1,0:T(8,128)(2,1)S(1)} %add_terms.19), channel_id=1, source_target_pairs={{0,4},{1,3},{4,8},{5,1},{8,12},{9,5},{12,14},{13,9},{14,10},{15,13... | collective-permute-start | bytes 1769480 | tf_op jit(solution)/shard_map/ppermute | solution.py:342
  333.8 24.0 %collective-permute-start.38 = (bf16[288,1024]{1,0:T(8,128)(2,1)S(1)}, bf16[288,1024]{1,0:T(8,128)(2,1)S(1)}, u32[]{:S(2)}, u32[]{:S(2)}) collective-permute-start(bf16[288,1024]{1,0:T(8,128)(2,1)S(1)} %add_terms.27), channel_id=1, source_target_pairs={{0,4},{1,3},{4,8},{5,1},{8,12},{9,5},{12,14},{13,9},{14,10},{15,13... | collective-permute-start | bytes 1769480 | tf_op jit(solution)/shard_map/ppermute | solution.py:342
  340.2 23.9 %collective-permute-start.32 = (bf16[288,1024]{1,0:T(8,128)(2,1)S(1)}, bf16[288,1024]{1,0:T(8,128)(2,1)S(1)}, u32[]{:S(2)}, u32[]{:S(2)}) collective-permute-start(bf16[288,1024]{1,0:T(8,128)(2,1)S(1)} %add_terms.20), channel_id=1, source_target_pairs={{0,4},{1,3},{4,8},{5,1},{8,12},{9,5},{12,14},{13,9},{14,10},{15,13... | collective-permute-start | bytes 1769480 | tf_op jit(solution)/shard_map/ppermute | solution.py:342
  344.9 19.1 %collective-permute-start.22 = (bf16[288,2048]{1,0:T(8,128)(2,1)S(1)}, bf16[288,2048]{1,0:T(8,128)(2,1)S(1)}, u32[]{:S(2)}, u32[]{:S(2)}) collective-permute-start(bf16[288,2048]{1,0:T(8,128)(2,1)S(1)} %get-tuple-element.124), channel_id=1, source_target_pairs={{0,1},{1,0},{2,3},{3,2},{4,5},{5,4},{6,7},{7,6},{8,9},{9,8},{10,11... | collective-permute-start | bytes 3538952 | tf_op jit(solution)/shard_map/ppermute | solution.py:333
  357.3 17.0 %collective-permute-start.21 = (bf16[288,2048]{1,0:T(8,128)(2,1)S(1)}, bf16[288,2048]{1,0:T(8,128)(2,1)S(1)}, u32[]{:S(2)}, u32[]{:S(2)}) collective-permute-start(bf16[288,2048]{1,0:T(8,128)(2,1)S(1)} %get-tuple-element.120), channel_id=1, source_target_pairs={{0,1},{1,0},{2,3},{3,2},{4,5},{5,4},{6,7},{7,6},{8,9},{9,8},{10,11... | collective-permute-start | bytes 3538952 | tf_op jit(solution)/shard_map/ppermute | solution.py:333
  358.1 9.9 %collective-permute-start.39 = (bf16[288,1024]{1,0:T(8,128)(2,1)S(1)}, bf16[288,1024]{1,0:T(8,128)(2,1)S(1)}, u32[]{:S(2)}, u32[]{:S(2)}) collective-permute-start(bf16[288,1024]{1,0:T(8,128)(2,1)S(1)} %add_terms.28), channel_id=1, source_target_pairs={{0,4},{1,3},{4,8},{5,1},{8,12},{9,5},{12,14},{13,9},{14,10},{15,13... | collective-permute-start | bytes 1769480 | tf_op jit(solution)/shard_map/ppermute | solution.py:342
  364.3 10.1 %collective-permute-start.33 = (bf16[288,1024]{1,0:T(8,128)(2,1)S(1)}, bf16[288,1024]{1,0:T(8,128)(2,1)S(1)}, u32[]{:S(2)}, u32[]{:S(2)}) collective-permute-start(bf16[288,1024]{1,0:T(8,128)(2,1)S(1)} %add_terms.21), channel_id=1, source_target_pairs={{0,4},{1,3},{4,8},{5,1},{8,12},{9,5},{12,14},{13,9},{14,10},{15,13... | collective-permute-start | bytes 1769480 | tf_op jit(solution)/shard_map/ppermute | solution.py:342
  364.8 17.8 %collective-permute-start.13 = (bf16[288,2048]{1,0:T(8,128)(2,1)S(1)}, bf16[288,2048]{1,0:T(8,128)(2,1)S(1)}, u32[]{:S(2)}, u32[]{:S(2)}) collective-permute-start(bf16[288,2048]{1,0:T(8,128)(2,1)S(1)} %get-tuple-element.106), channel_id=1, source_target_pairs={{0,1},{1,0},{2,3},{3,2},{4,5},{5,4},{6,7},{7,6},{8,9},{9,8},{10,11... | collective-permute-start | bytes 3538952 | tf_op jit(solution)/shard_map/ppermute | solution.py:333
  368.2 12.4 %collective-permute-start.40 = (bf16[288,1024]{1,0:T(8,128)(2,1)S(1)}, bf16[288,1024]{1,0:T(8,128)(2,1)S(1)}, u32[]{:S(2)}, u32[]{:S(2)}) collective-permute-start(bf16[288,1024]{1,0:T(8,128)(2,1)S(1)} %add_terms.29), channel_id=1, source_target_pairs={{0,4},{1,3},{4,8},{5,1},{8,12},{9,5},{12,14},{13,9},{14,10},{15,13... | collective-permute-start | bytes 1769480 | tf_op jit(solution)/shard_map/ppermute | solution.py:342
  374.6 12.4 %collective-permute-start.34 = (bf16[288,1024]{1,0:T(8,128)(2,1)S(1)}, bf16[288,1024]{1,0:T(8,128)(2,1)S(1)}, u32[]{:S(2)}, u32[]{:S(2)}) collective-permute-start(bf16[288,1024]{1,0:T(8,128)(2,1)S(1)} %add_terms.22), channel_id=1, source_target_pairs={{0,4},{1,3},{4,8},{5,1},{8,12},{9,5},{12,14},{13,9},{14,10},{15,13... | collective-permute-start | bytes 1769480 | tf_op jit(solution)/shard_map/ppermute | solution.py:342
  380.9 12.4 %collective-permute-start.41 = (bf16[288,1024]{1,0:T(8,128)(2,1)S(1)}, bf16[288,1024]{1,0:T(8,128)(2,1)S(1)}, u32[]{:S(2)}, u32[]{:S(2)}) collective-permute-start(bf16[288,1024]{1,0:T(8,128)(2,1)S(1)} %add_terms.30), channel_id=1, source_target_pairs={{0,4},{1,3},{4,8},{5,1},{8,12},{9,5},{12,14},{13,9},{14,10},{15,13... | collective-permute-start | bytes 1769480 | tf_op jit(solution)/shard_map/ppermute | solution.py:342
  393.6 2.1 collective-permute-start.42
  (8 other events, 32.9 us)
